TPU v7x, 128 devices: a whole 4x4x4 slice. The times are simulated.
128 devices in a mesh: dp: 2 (over core), row: 4 (over x), col: 16 (over z, y).
Axes of the slice: x: 4, y: 4, z: 4, core: 2. Of those that a mesh axis runs over, the one named last changes fastest.
Arguments:
- inputs: bfloat16 [768, 16384], P('col', ('dp', 'row')), may hold values from -6 to 6
- segments: int32 [2, 8192], P('dp'), may hold values from 0 to 4, as said below
- joint_weight: bfloat16 [768, 2304], P('col', 'row'), may hold values from -0.21875 to 0.21875
- joint_bias: float32 [1536], P('row'), may hold values from -1.8 to 1.8
- output_weight: bfloat16 [768, 768], P('row', 'col'), may hold values from -6 to 6
- output_bias: float32 [768], P('col'), may hold values from -1.8 to 1.8
- first_norm_gain: float32 [768], P('col'), may hold values from 0.5 to 1.5
- shift_first: float32 [768], P('col'), may hold values from -1.8 to 1.8
- up_weight: bfloat16 [768, 3072], P('col', 'row'), may hold values from -0.21875 to 0.21875
- up_bias: float32 [3072], P('row'), may hold values from -1.8 to 1.8
- down_weight: bfloat16 [768, 3072], P('col', 'row'), may hold values from -0.109375 to 0.109375
- down_bias: float32 [768], P('col'), may hold values from -1.8 to 1.8
- second_norm_gain: float32 [768], P('col'), may hold values from 0.5 to 1.5
- second_norm_shift: float32 [768], P('col'), may hold values from -1.8 to 1.8
- cotangent: bfloat16 [768, 16384], P('col', ('dp', 'row')), may hold values from -6 to 6
Outputs:
- layer_output: bfloat16 [768, 16384], P('col', ('dp', 'row'))
- grad_inputs: float32 [768, 16384], P('col', ('dp', 'row'))
- grad_joint_weight: float32 [768, 2304], P('col', 'row')
- grad_joint_bias: float32 [1536], P('row')
- grad_output_weight: float32 [768, 768], P('row', 'col')
- grad_output_bias: float32 [768], P('col')
- grad_gain_first: float32 [768], P('col')
- grad_shift_first: float32 [768], P('col')
- grad_up_weight: float32 [768, 3072], P('col', 'row')
- grad_up_bias: float32 [3072], P('row')
- grad_down_weight: float32 [768, 3072], P('col', 'row')
- grad_down_bias: float32 [768], P('col')
- grad_gain_second: float32 [768], P('col')
- grad_shift_second: float32 [768], P('col')
Inputs may be any that keep to these rules, and one draw needn't show every extreme that they name: `segments`: in every sequence the segment numbers start at 0, rise by 0 or 1 from one token to the next, and end at 4.
All inputs are finite; a program needn't handle non-finite values.
Results may differ from a plain program's by a relative error of at most 0.019.
Values may be sent and summed in bfloat16 or wider, within the bound.
No kernel may reach another device: no remote copies, remote signals or barrier semaphores. Data moves between devices by JAX's collectives and lax.ppermute only.
A program may use at most 128 MiB of HBM per device.

v0:
```python
import math

import jax
import jax.numpy as jnp
from jax import lax
from jax.experimental import pallas as pl
from jax.experimental.pallas import tpu as pltpu
from jax.sharding import PartitionSpec as P

HDIM = 64
EPS = 1e-06
BLOCK_OUT = -1e30
LOG2E = 1.4426950408889634
BF = jnp.bfloat16
F32 = jnp.float32

DIM = 768
FF = 3072
NCOL = 16
NROW = 4
TOK = 128
PER_HEAD = 5
SHARE = 26
SLOTS = NROW * NCOL
ROWS = SLOTS * SHARE
AUG = 144
JW = 640
HALF = 2
FWD_C = 2
BWD_C = 2
Q_AT = NROW * TOK
C_AT = Q_AT + 64
BLOCK = C_AT + 48
MIB = 2**20
COL = ("z", "y")
ALL = ("row", "z", "y")
VMEM = pl.BlockSpec(memory_space=pltpu.VMEM)
SMEM = pl.BlockSpec(memory_space=pltpu.SMEM)
A_AT = 5 * DIM + 48
SENT = A_AT + 192
SAME = 3 * DIM + 48
WROWS = 768


def split3(v):
    hi = v.astype(BF)
    rest = v - hi.astype(F32)
    mid = rest.astype(BF)
    low = (rest - mid.astype(F32)).astype(BF)
    return hi, mid, low


def dot(a, b, ca, cb):
    return lax.dot_general(a, b, (((ca,), (cb,)), ((), ())), preferred_element_type=F32)


LIMITS = {
    "project": 16,
    "attend": 32,
    "attend_back_first": 63.9,
    "attend_back_second": 63.9,
    "tokenwise": 63.9,
    "weight_grads": 63.9,
    "project_back": 63.9,
    "last_payload": 12,
    "finish": 12,
    "joint_gradient": 8,
}


def params(name):
    return pltpu.CompilerParams(vmem_limit_bytes=int(LIMITS[name] * MIB))


def cost(us):
    return pl.CostEstimate(flops=int(us * 1e9), bytes_accessed=int(us * 2e6), transcendentals=0)


Q_BLOCK = pl.BlockSpec((NCOL, 64, 128), lambda i: (0, Q_AT // 64, 0))


def whole(shape):
    return pl.BlockSpec(shape, lambda i: (0,) * len(shape))


def pack(ref, at, lane, scale=None):
    lanes = slice(lane, lane + HDIM)
    rest = jnp.concatenate([ref[at + 16 : at + SHARE, lanes], jnp.zeros((6, HDIM), F32)], axis=0)
    both = jnp.concatenate([ref[at : at + 16, lanes], rest], axis=1)
    return (both if scale is None else both * scale).astype(BF)


def unpack(block, ref, at, lane, rows=SHARE):
    block = block.astype(F32)
    lanes = slice(lane, lane + HDIM)
    ref[at : at + 16, lanes] = block[:, 0:64]
    ref[at + 16 : at + rows, lanes] = block[0 : rows - 16, 64:128]


def project_kernel(x_ref, w_ref, b_ref, cot_ref, out_ref, q_ref):
    w = w_ref[...].reshape(DIM, JW)
    q_ref[...] = jnp.zeros_like(q_ref)
    for r in range(NROW):
        tokens = x_ref[r].astype(F32).T.astype(BF)
        y = dot(tokens, w, 1, 0) + b_ref[...]
        q_ref[r * TOK : (r + 1) * TOK, :] = y[:, 0:256]
        for h in range(3):
            kv = y[:, 256 + 128 * h : 384 + 128 * h].T.astype(BF)
            for j in range(PER_HEAD * h, PER_HEAD * (h + 1) + (1 if h == 2 else 0)):
                out_ref[j, r * TOK : (r + 1) * TOK, :] = kv
    for j in range(NCOL):
        h, k = min(j, 14) // PER_HEAD, min(j, 14) % PER_HEAD
        for r in range(NROW):
            at = r * TOK + SHARE * k
            out_ref[j, Q_AT + 16 * r : Q_AT + 16 * (r + 1), :] = pack(q_ref, at, HDIM * h)
    out_ref[:, C_AT:BLOCK, :] = cot_ref[...]


def project(x4, wj, bias, cot):
    return pl.pallas_call(
        project_kernel,
        out_shape=pltpu.HBM((NCOL, BLOCK, 128), BF),
        in_specs=[VMEM] * 4,
        out_specs=VMEM,
        scratch_shapes=[pltpu.VMEM((640, 256), F32)],
        compiler_params=params("project"),
        cost_estimate=cost(3),
        name="project",
    )(x4, wj, bias, cot)


def key_rows(seg_row):
    row = lax.broadcasted_iota(jnp.int32, (16, seg_row.shape[1]), 0)
    hot = jnp.where(row < 5, jnp.where(row == seg_row, 1.0, 0.0), jnp.where(row < 8, 1.0, 0.0))
    return hot.astype(BF)


def offset_columns(value, base):
    h, m, l = split3(-value)
    lane = lax.broadcasted_iota(jnp.int32, base.shape, 1)
    return jnp.where(
        lane == 5,
        h.astype(F32),
        jnp.where(lane == 6, m.astype(F32), jnp.where(lane == 7, l.astype(F32), base)),
    )


def key_block(kv_ref, seg_ref, begin):
    pairs = [(c, r) for c in range(kv_ref.shape[0]) for r in range(kv_ref.shape[1] // TOK)]
    tiles = [kv_ref[c, r * TOK : (r + 1) * TOK, :] for c, r in pairs]
    at = pl.program_id(0) * kv_ref.shape[0]
    extra = [key_rows(seg_ref[pl.ds((begin + r) * NCOL + at + c, 1), :]) for c, r in pairs]
    return jnp.concatenate(tiles, axis=1), jnp.concatenate(extra, axis=1)


def forward_step(qa_ref, kv_ref, seg_ref, acc_ref, top_ref):
    kvt, extra = key_block(kv_ref, seg_ref, 0)
    kt = jnp.concatenate([kvt[0:64], kvt[0:64], extra], axis=0)
    turned = kvt.astype(F32).T
    lane = lax.broadcasted_iota(jnp.int32, turned.shape, 1)
    va = jnp.where(lane >= 64, turned, jnp.where(lane == 0, 1.0, 0.0)).astype(BF)
    s = dot(qa_ref[...], kt, 1, 0)
    parts = [s[:, i * 128 : (i + 1) * 128] for i in range(s.shape[1] // 128)]
    high = parts[0]
    for part in parts[1:]:
        high = jnp.maximum(high, part)
    top = top_ref[...]
    raised = jnp.maximum(top, jnp.broadcast_to(jnp.max(high, axis=1, keepdims=True), top.shape))
    p = jnp.concatenate([jnp.exp2(part - raised).astype(BF) for part in parts], axis=1)
    fade = jnp.exp2(top - raised)
    top_ref[...] = raised
    acc_ref[...] = acc_ref[...] * fade + dot(p, va, 1, 0)


def attend_kernel(
    shift_ref, q_ref, kv_ref, seg_ref, qa_ref, o_ref, out_ref, q_scr, pen_scr, acc_ref, top_ref
):
    @pl.when(pl.program_id(0) == 0)
    def _():
        columns = pltpu.roll(seg_ref[...].astype(F32), shift_ref[0], 1).T
        lane = lax.broadcasted_iota(jnp.int32, (SHARE, 16), 1)
        seg = lane.astype(F32)
        for r in range(NROW):
            for c in range(NCOL):
                slot = r * NCOL + c
                unpack(q_ref[c, 16 * r : 16 * (r + 1), :], q_scr, SHARE * slot, 0)
                pen_scr[SHARE * slot : SHARE * (slot + 1), :] = jnp.where(
                    (lane < 5) & (seg != columns[0:SHARE, slot : slot + 1]), BLOCK_OUT, 0.0
                )
        scaled = q_scr[...] * (LOG2E / 8.0)
        hi = scaled.astype(BF)
        lo = (scaled - hi.astype(F32)).astype(BF)
        pen = pen_scr[...]
        qa_ref[...] = jnp.concatenate([hi, lo, pen.astype(BF)], axis=1)
        acc_ref[...] = jnp.zeros_like(acc_ref)
        top_ref[...] = jnp.full_like(top_ref, -3e38)

    forward_step(qa_ref, kv_ref, seg_ref, acc_ref, top_ref)

    @pl.when(pl.program_id(0) == pl.num_programs(0) - 1)
    def _():
        acc = acc_ref[...]
        total = acc[:, 0:1]
        o_ref[...] = acc[:, 64:128] / total
        lse = top_ref[:, 0:1] + jnp.log(total) * LOG2E
        qa_ref[:, 128:144] = offset_columns(lse, qa_ref[:, 128:144].astype(F32)).astype(BF)
        for slot in range(SLOTS):
            out_ref[slot] = pack(o_ref, SHARE * slot, 0)


def attend(shift, arrived, seg):
    return pl.pallas_call(
        attend_kernel,
        grid=(NCOL // FWD_C,),
        out_shape=(
            pltpu.HBM((ROWS, AUG), BF),
            pltpu.HBM((ROWS, HDIM), F32),
            pltpu.HBM((SLOTS, 16, 128), BF),
        ),
        in_specs=[
            SMEM,
            Q_BLOCK,
            pl.BlockSpec((FWD_C, Q_AT, 128), lambda i: (i, 0, 0)),
            whole((SLOTS, TOK)),
        ],
        out_specs=[whole((ROWS, AUG)), whole((ROWS, HDIM)), whole((SLOTS, 16, 128))],
        scratch_shapes=[
            pltpu.VMEM((ROWS, HDIM), F32),
            pltpu.VMEM((ROWS, 16), F32),
            pltpu.VMEM((ROWS, 128), F32),
            pltpu.VMEM((ROWS, 128), F32),
        ],
        compiler_params=params("attend"),
        cost_estimate=cost(20),
        name="attend",
    )(shift, arrived, arrived, seg)


def backward_step(qa_ref, doa_ref, turned_ref, kv_ref, seg_ref, begin, acc_ref):
    kvt, extra = key_block(kv_ref, seg_ref, begin)
    kt = jnp.concatenate([kvt[0:64], kvt[0:64], extra], axis=0)
    vt = jnp.concatenate([kvt[64:128], extra], axis=0)
    keys = kvt.astype(F32).T.astype(BF)
    p = jnp.exp2(dot(qa_ref[...], kt, 1, 0))
    dp = dot(doa_ref[...], vt, 1, 0)
    ds = (p * dp).astype(BF)
    acc_ref[...] += dot(ds, keys, 1, 0)
    dk = dot(turned_ref[0:64, :], ds, 1, 0) * 0.125
    dv = dot(turned_ref[64:128, :], p.astype(BF), 1, 0)
    return jnp.concatenate([dk, dv], axis=0).astype(BF)


def store_keys(out_ref, at, both):
    for c in range(BWD_C):
        for r in range(HALF):
            i = c * HALF + r
            out_ref[at + c, r * TOK : (r + 1) * TOK, :] = both[:, i * TOK : (i + 1) * TOK]


def back_first_kernel(
    q_ref, do_ref, qa_ref, o_ref, fin_ref, kv_ref, seg_ref, out_ref, doa_ref, turned_ref, acc_ref, pair_scr
):
    @pl.when(pl.program_id(0) == 0)
    def _():
        for r in range(NROW):
            for c in range(NCOL):
                slot = r * NCOL + c
                unpack(q_ref[c, 16 * r : 16 * (r + 1), :], pair_scr, SHARE * slot, 0)
                unpack(do_ref[slot], pair_scr, SHARE * slot, HDIM)
        pairs = pair_scr[...]
        turned_ref[...] = pairs.T.astype(BF)
        grad = pairs[:, 64:128]
        delta = jnp.sum(grad * o_ref[...], axis=1, keepdims=True)
        ext = offset_columns(delta, jnp.zeros((ROWS, 16), F32))
        doa_ref[...] = jnp.concatenate([grad.astype(BF), ext.astype(BF)], axis=1)
        acc_ref[...] = jnp.zeros_like(acc_ref)

    both = backward_step(qa_ref, doa_ref, turned_ref, kv_ref, seg_ref, 0, acc_ref)
    store_keys(out_ref, 0, both)
    out_ref[:, 256:304, :] = fin_ref[...]


def back_second_kernel(
    qa_ref, doa_ref, turned_ref, acc_in, kv_ref, seg_ref, out_ref, acc_ref
):
    step = pl.program_id(0)

    @pl.when(step == 0)
    def _():
        acc_ref[...] = acc_in[...]

    both = backward_step(qa_ref, doa_ref, turned_ref, kv_ref, seg_ref, HALF, acc_ref)
    store_keys(out_ref, step * BWD_C, both)

    @pl.when(step == pl.num_programs(0) - 1)
    def _():
        for r in range(NROW):
            for c in range(NCOL):
                block = pack(acc_ref, SHARE * (r * NCOL + c), 0, 0.125)
                out_ref[c, 256 + 16 * r : 272 + 16 * r, :] = block


SEG_BACK = whole((SLOTS, TOK))
BACK_STEPS = NCOL // BWD_C


def attend_back_first(arrived, grad, qa, o, fin, seg):
    return pl.pallas_call(
        back_first_kernel,
        grid=(BACK_STEPS,),
        out_shape=(
            pltpu.HBM((NCOL, 304, 128), BF),
            pltpu.HBM((ROWS, 80), BF),
            pltpu.HBM((128, ROWS), BF),
            pltpu.HBM((ROWS, 128), F32),
        ),
        in_specs=[
            Q_BLOCK,
            whole((SLOTS, 16, 128)),
            whole((ROWS, AUG)),
            whole((ROWS, HDIM)),
            pl.BlockSpec((BWD_C, 48, 128), lambda i: (i, 0, 0)),
            pl.BlockSpec((BWD_C, HALF * TOK, 128), lambda i: (i, 0, 0)),
            SEG_BACK,
        ],
        out_specs=[
            pl.BlockSpec((BWD_C, 304, 128), lambda i: (i, 0, 0)),
            whole((ROWS, 80)),
            whole((128, ROWS)),
            whole((ROWS, 128)),
        ],
        scratch_shapes=[pltpu.VMEM((ROWS, 128), F32)],
        compiler_params=params("attend_back_first"),
        cost_estimate=cost(18),
        name="attend_back_first",
    )(arrived, grad, qa, o, fin, arrived, seg)


def attend_back_second(qa, doa, turned, acc, arrived, seg):
    return pl.pallas_call(
        back_second_kernel,
        grid=(BACK_STEPS,),
        out_shape=pltpu.HBM((NCOL, 320, 128), BF),
        in_specs=[
            whole((ROWS, AUG)),
            whole((ROWS, 80)),
            whole((128, ROWS)),
            whole((ROWS, 128)),
            pl.BlockSpec((BWD_C, HALF * TOK, 128), lambda i: (i, 1, 0)),
            SEG_BACK,
        ],
        out_specs=whole((NCOL, 320, 128)),
        scratch_shapes=[pltpu.VMEM((ROWS, 128), F32)],
        compiler_params=params("attend_back_second"),
        cost_estimate=cost(18),
        name="attend_back_second",
    )(qa, doa, turned, acc, arrived, seg)


def heads_of(block):
    return jnp.concatenate(
        [
            jnp.concatenate([block[64 * h : 64 * (h + 1), 64 * k : 64 * (k + 1)] for h in range(3)], axis=1)
            for k in range(2)
        ],
        axis=0,
    )


def room(k):
    return min(SHARE, TOK - SHARE * k)


def feature_mean(v):
    return jnp.sum(v, axis=1, keepdims=True) * (1.0 / DIM)


def tokenwise_kernel(
    row_ref, att_ref, x_ref, cot_ref, vec_ref, upb_ref, all_ref,
    same_ref, sent_ref, datt_ref, fin_ref, dh1_ref,
    up_ref, down_ref, out_ref, slope_ref, att_scr, back_scr, sems,
):
    row = row_ref[0]
    copies = []
    for g in range(3):
        for k in range(2):
            for r in range(NROW):
                copies.append(
                    pltpu.make_async_copy(
                        all_ref.at[k, r, :, 96:112, g * 128 : (g + 1) * 128],
                        out_ref.at[k * NROW + r, :, 16 * g : 16 * (g + 1), :],
                        sems.at[0],
                    )
                )
    n_out = len(copies)
    for r in range(NROW):
        for k in range(2):
            lanes = slice(r * DIM + k * 384, r * DIM + (k + 1) * 384)
            copies.append(
                pltpu.make_async_copy(all_ref.at[k, r, :, 0:48, :], up_ref.at[:, :, lanes], sems.at[1 + r])
            )
    for r in range(NROW):
        for k in range(2):
            lanes = slice(r * DIM + k * 384, r * DIM + (k + 1) * 384)
            copies.append(
                pltpu.make_async_copy(all_ref.at[k, r, :, 48:96, :], down_ref.at[:, :, lanes], sems.at[5 + r])
            )
    for copy in copies:
        copy.start()

    def wait(group):
        chosen = copies[:n_out] if group == 0 else copies[n_out + 2 * (group - 1) : n_out + 2 * group]
        for copy in chosen:
            copy.wait()

    tok = x_ref[...].reshape(DIM, TOK).astype(F32).T
    cot = cot_ref[...].reshape(DIM, TOK).astype(F32).T
    vecs = vec_ref[...].reshape(DIM, TOK).astype(F32).T[64:128]
    out_b, gain_1, shift_1, down_b, gain_2, shift_2 = [
        vecs[i : i + 1] + vecs[6 + i : 7 + i] + vecs[12 + i : 13 + i] for i in range(6)
    ]
    gap = jnp.zeros((TOK, 32), BF)

    for r in range(NROW):
        for j in range(15):
            h, k = j // PER_HEAD, j % PER_HEAD
            unpack(att_ref[r * NCOL + j], att_scr, SHARE * k, 192 * r + HDIM * h, room(k))
    for r in range(NROW):
        target = lax.rem(r + NROW - row, NROW)
        for h in range(3):
            lanes = slice(192 * r + HDIM * h, 192 * r + HDIM * (h + 1))
            both = jnp.concatenate([att_scr[0:64, lanes], att_scr[64:128, lanes]], axis=1)
            at = A_AT - SAME + 64 * h
            sent_ref[target, at : at + 64, :] = both.astype(BF)
    wait(0)
    attn = jnp.zeros((TOK, DIM), F32)
    for r in range(NROW):
        for k in range(2):
            lanes = slice(192 * r + 96 * k, 192 * r + 96 * (k + 1))
            piece = jnp.concatenate([att_scr[:, lanes].astype(BF), gap], axis=1)
            attn = attn + dot(piece, out_ref[k * NROW + r].reshape(DIM, 128), 1, 1)
    h1 = tok + (attn + out_b)
    off = h1 - feature_mean(h1)
    inv1 = lax.rsqrt(feature_mean(off * off) + EPS)
    xhat1 = off * inv1
    n1 = xhat1 * gain_1 + shift_1
    n1_low = n1.astype(BF)

    branch = jnp.zeros((TOK, DIM), F32)
    for r in range(NROW):
        wait(1 + r)
        cols = slice(r * DIM, (r + 1) * DIM)
        pre = dot(n1_low, up_ref[:, :, cols].reshape(DIM, DIM), 1, 0) + upb_ref[r : r + 1, :]
        phi = 0.5 * (1.0 + lax.erf(pre * (1.0 / math.sqrt(2.0))))
        act = (pre * phi).astype(BF)
        slope_ref[:, cols] = phi + pre * jnp.exp(-0.5 * pre * pre) * (1.0 / math.sqrt(2.0 * math.pi))
        for i in range(6):
            at = DIM + i * TOK
            sent_ref[lax.rem(r + NROW - row, NROW), at : at + TOK, :] = act[:, i * TOK : (i + 1) * TOK]
        wait(5 + r)
        branch = branch + dot(act, down_ref[:, :, cols].reshape(DIM, DIM), 1, 1)
    h2 = n1 + (branch + down_b)
    off = h2 - feature_mean(h2)
    inv2 = lax.rsqrt(feature_mean(off * off) + EPS)
    xhat2 = off * inv2
    fin_ref[...] = (xhat2 * gain_2 + shift_2).T.astype(BF).reshape(NCOL, 48, TOK)
    dx = cot * gain_2
    dh2 = inv2 * (dx - feature_mean(dx) - xhat2 * feature_mean(dx * xhat2))
    d_branch = dh2.astype(BF)

    back = jnp.zeros((TOK, DIM), F32)
    for r in range(NROW):
        cols = slice(r * DIM, (r + 1) * DIM)
        d_act = dot(d_branch, down_ref[:, :, cols].reshape(DIM, DIM), 1, 0)
        d_pre = (d_act * slope_ref[:, cols]).astype(BF)
        for i in range(6):
            at = i * TOK
            sent_ref[lax.rem(r + NROW - row, NROW), at : at + TOK, :] = d_pre[:, i * TOK : (i + 1) * TOK]
        back = back + dot(d_pre, up_ref[:, :, cols].reshape(DIM, DIM), 1, 1)
    up1 = dh2 + back
    dx = up1 * gain_1
    dh1 = inv1 * (dx - feature_mean(dx) - xhat1 * feature_mean(dx * xhat1))
    d_attn = dh1.astype(BF)
    back_scr[TOK : TOK + 8, :] = jnp.zeros((8, 192), F32)
    for r in range(NROW):
        pieces = [dot(d_attn, out_ref[k * NROW + r].reshape(DIM, 128), 1, 0)[:, 0:96] for k in range(2)]
        back_scr[0:TOK, :] = jnp.concatenate(pieces, axis=1)
        for j in range(15):
            h, k = j // PER_HEAD, j % PER_HEAD
            datt_ref[r * NCOL + j] = pack(back_scr, SHARE * k, HDIM * h)
        datt_ref[r * NCOL + 15] = jnp.zeros((16, 128), BF)
    turned = dh1.T
    dh1_ref[...] = turned
    shared = [n1.T.astype(BF), dh2.T.astype(BF), turned.astype(BF)]
    sums = [
        jnp.sum(v, axis=0, keepdims=True) for v in (up1 * xhat1, up1, cot * xhat2, cot)
    ]
    rows = []
    for part in range(2):
        for v in sums:
            hi = v.astype(BF).astype(F32)
            piece = hi if part == 0 else v - hi
            rows += [piece[:, i * 128 : (i + 1) * 128] for i in range(6)]
    shared.append(jnp.concatenate(rows, axis=0).astype(BF))
    at = 0
    for v in shared:
        same_ref[at : at + v.shape[0], :] = v
        at += v.shape[0]


def tokenwise(row, att, x_t, arrived, wj, up_bias, everything):
    return pl.pallas_call(
        tokenwise_kernel,
        out_shape=(
            pltpu.HBM((SAME, TOK), BF),
            pltpu.HBM((NROW, SENT - SAME, TOK), BF),
            pltpu.HBM((SLOTS, 16, 128), BF),
            pltpu.HBM((NCOL, 48, TOK), BF),
            pltpu.HBM((DIM, TOK), F32),
        ),
        grid=(1,),
        in_specs=[
            SMEM,
            whole((SLOTS, 16, 128)),
            whole((NCOL, 48, TOK)),
            pl.BlockSpec((NCOL, 48, TOK), lambda i: (0, C_AT // 48, 0)),
            pl.BlockSpec((NCOL, 48, TOK), lambda i: (0, 0, 1)),
            whole((NROW, DIM)),
            pl.BlockSpec(memory_space=pl.ANY),
        ],
        out_specs=[
            whole((SAME, TOK)),
            whole((NROW, SENT - SAME, TOK)),
            whole((SLOTS, 16, 128)),
            whole((NCOL, 48, TOK)),
            whole((DIM, TOK)),
        ],
        scratch_shapes=[
            pltpu.VMEM((NCOL, 48, FF), BF),
            pltpu.VMEM((NCOL, 48, FF), BF),
            pltpu.VMEM((2 * NROW, NCOL, 48, 128), BF),
            pltpu.VMEM((TOK, FF), F32),
            pltpu.VMEM((TOK, DIM), F32),
            pltpu.VMEM((TOK + 8, 192), F32),
            pltpu.SemaphoreType.DMA((9,)),
        ],
        compiler_params=params("tokenwise"),
        cost_estimate=cost(15),
        name="tokenwise",
    )(row, att, x_t, arrived, wj, up_bias, everything)


def weight_grads_kernel(core_ref, *refs):
    got, out_ref = refs[:-1], refs[-1]

    def feats(at):
        return jnp.concatenate([ref[at : at + DIM, :] for ref in got], axis=1)

    def hidden(at, begin, end):
        return jnp.concatenate(
            [
                jnp.concatenate(
                    [ref[at + i * TOK : at + (i + 1) * TOK, :] for i in range(begin, end)], axis=1
                )
                for ref in got
            ],
            axis=0,
        )

    def keep(at, g):
        for i in range(g.shape[1] // 128):
            piece = g[:, i * 128 : (i + 1) * 128].astype(BF).reshape(NCOL, 48, 128)
            out_ref[:, at + 48 * i : at + 48 * (i + 1), :] = piece

    @pl.when(core_ref[0] == 0)
    def _():
        keep(0, dot(feats(0), hidden(3 * DIM + 48, 0, 6), 1, 0))
        keep(288, dot(feats(DIM), hidden(4 * DIM + 48, 0, 2), 1, 0))

    @pl.when(core_ref[0] != 0)
    def _():
        d_branch = feats(DIM)
        d_attn = feats(2 * DIM)
        keep(0, dot(d_branch, hidden(4 * DIM + 48, 2, 6), 1, 0))
        att = [heads_of(ref[A_AT:SENT, :].astype(F32)).astype(BF) for ref in got]
        att = jnp.concatenate(att, axis=0)
        att = jnp.concatenate([att, jnp.zeros((att.shape[0], 64), BF)], axis=1)
        keep(192, dot(d_attn, att, 1, 0))
        d_pre = hidden(3 * DIM + 48, 0, 6)
        ones = jnp.ones((16, d_pre.shape[0]), BF)
        sums = [dot(ones, d_branch, 1, 1)[0:1], dot(ones, d_attn, 1, 1)[0:1], dot(ones, d_pre, 1, 0)[0:1]]
        norm = got[0][3 * DIM : 3 * DIM + 48, :].astype(F32)
        for ref in got[1:]:
            norm = norm + ref[3 * DIM : 3 * DIM + 48, :].astype(F32)
        rows = [norm[0:24] + norm[24:48]]
        for v in sums:
            rows += [v[:, i * 128 : (i + 1) * 128] for i in range(6)]
        rows.append(jnp.zeros((6, 128), F32))
        rows = jnp.concatenate(rows, axis=0)
        hi = rows.astype(BF)
        lo = (rows - hi.astype(F32)).astype(BF)
        misc = jnp.concatenate([hi, lo], axis=0)
        out_ref[:, 288:384, :] = jnp.broadcast_to(misc[None], (NCOL, 96, 128))


def weight_grads(core, got, theirs):
    shape = (NCOL, WROWS // 2, 128)
    return pl.pallas_call(
        weight_grads_kernel,
        grid=(1,),
        out_shape=pltpu.HBM(shape, BF),
        in_specs=[SMEM] + [whole((SENT, TOK))] * 8,
        out_specs=whole(shape),
        compiler_params=params("weight_grads"),
        cost_estimate=cost(1),
        name="weight_grads",
    )(core, *got, *theirs)


def place(core, mine_ref, other_ref, blocks, half_rows):
    for at, block in blocks:
        low = at < half_rows
        local = at if low else at - half_rows
        rows = slice(local, local + block.shape[1])
        keep = core == (0 if low else 1)

        @pl.when(keep)
        def _():
            mine_ref[:, rows, :] = block

        @pl.when(jnp.logical_not(keep))
        def _():
            other_ref[:, rows, :] = block


def project_back_kernel(
    core_ref, first_ref, second_ref, w_ref, x_ref, din_ref, mine_ref, other_ref, layer_ref, scr
):
    core = core_ref[0]
    layer_ref[...] = jnp.concatenate([first_ref[c, 256:304, :] for c in range(NCOL)], axis=1)
    scr[...] = jnp.zeros_like(scr)
    for j in range(15):
        h, k = j // PER_HEAD, j % PER_HEAD
        for r in range(NROW):
            block = second_ref[j, 256 + 16 * r : 272 + 16 * r, :]
            unpack(block, scr, r * TOK + SHARE * k, HDIM * h, room(k))
    dq = scr[...].T.astype(BF)
    w = w_ref[...].reshape(DIM, JW)
    grad = jnp.zeros((DIM, JW), F32)
    total = jnp.zeros((16, JW), F32)
    ones = jnp.ones((16, TOK), BF)
    for r in range(NROW):
        source, at = (first_ref, r) if r < HALF else (second_ref, r - HALF)
        parts = [dq[:, r * TOK : (r + 1) * TOK]]
        for h in range(3):
            acc = source[PER_HEAD * h, at * TOK : (at + 1) * TOK, :].astype(F32)
            for k in range(1, PER_HEAD):
                acc = acc + source[PER_HEAD * h + k, at * TOK : (at + 1) * TOK, :].astype(F32)
            parts.append(acc.astype(BF))
        d_proj = jnp.concatenate(parts, axis=0)
        din_ref[r] = dot(w, d_proj, 1, 0).astype(BF)
        grad = grad + dot(x_ref[r], d_proj, 1, 1)
        total = total + dot(ones, d_proj, 1, 1)
    rows = [total[0:1, i * 128 : (i + 1) * 128] for i in range(5)] + [jnp.zeros((3, 128), F32)]
    rows = jnp.concatenate(rows, axis=0)
    hi = rows.astype(BF)
    lo = (rows - hi.astype(F32)).astype(BF)
    misc = jnp.broadcast_to(jnp.concatenate([hi, lo], axis=0)[None], (NCOL, 16, 128))
    low = grad.astype(BF)
    pieces = [low[:, i * 128 : (i + 1) * 128].reshape(NCOL, 48, 128) for i in range(5)]
    blocks = [(0, pieces[0]), (48, pieces[1]), (96, pieces[2][:, 0:32]), (128, pieces[2][:, 32:48])]
    blocks += [(144, pieces[3]), (192, pieces[4]), (240, misc)]
    place(core, mine_ref, other_ref, blocks, 128)


def project_back(core, first, second, wj, x4):
    kind = pltpu.HBM((NCOL, 128, 128), BF)
    return pl.pallas_call(
        project_back_kernel,
        out_shape=(
            pltpu.HBM((NROW, DIM, TOK), BF),
            kind,
            kind,
            pltpu.HBM((48, NCOL * TOK), BF),
        ),
        in_specs=[SMEM] + [VMEM] * 4,
        out_specs=[VMEM] * 4,
        scratch_shapes=[pltpu.VMEM((512, 256), F32)],
        compiler_params=params("project_back"),
        cost_estimate=cost(5),
        name="project_back",
    )(core, first, second, wj, x4)


def last_kernel(mine_ref, theirs_ref, din_ref, dh1_ref, out_ref):
    out_ref[:, 0:128, :] = (mine_ref[...].astype(F32) + theirs_ref[...].astype(F32)).astype(BF)
    total = dh1_ref[...]
    for r in range(NROW):
        total = total + din_ref[r].astype(F32)
    out_ref[:, 128:176, :] = total.astype(BF).reshape(NCOL, 48, TOK)


def last_payload(mine, theirs, din, dh1):
    return pl.pallas_call(
        last_kernel,
        out_shape=pltpu.HBM((NCOL, 176, 128), BF),
        in_specs=[VMEM] * 4,
        out_specs=VMEM,
        compiler_params=params("last_payload"),
        cost_estimate=cost(1),
        name="last_payload",
    )(mine, theirs, din, dh1)


def join(core_ref, mine, theirs):
    first = core_ref[0] == 0
    a, b = mine[...], theirs[...]
    return jnp.concatenate([jnp.where(first, a, b), jnp.where(first, b, a)], axis=0)


def finish_kernel(
    core_ref, col_ref, wide_ref, other_ref, out_ref, up_ref, up_bias_ref, down_ref, *own_refs
):
    wide = join(core_ref, wide_ref, other_ref)
    for i in range(6):
        lanes = slice(i * 128, (i + 1) * 128)
        up_ref[:, lanes] = wide[48 * i : 48 * (i + 1)]
        down_ref[:, lanes] = wide[288 + 48 * i : 288 + 48 * (i + 1)]
    out_ref[...] = jnp.concatenate([wide[576:624], wide[624:672, 0:64]], axis=1)
    vecs = wide[672:720] + wide[720:768]
    up_bias_ref[...] = vecs[36:42]
    rows = [
        jnp.concatenate([vecs[6 * v + i : 6 * v + i + 1] for i in range(6)], axis=1) for v in range(6)
    ]
    rows = jnp.concatenate(rows + [jnp.zeros((2, DIM), F32)], axis=0)
    feature = lax.broadcasted_iota(jnp.int32, (DIM, 48), 0)
    lane = lax.broadcasted_iota(jnp.int32, (DIM, 48), 1)
    pick = jnp.where(feature == col_ref[0] * 48 + lane, 1.0, 0.0).astype(BF)
    own = sum(dot(part, pick, 1, 0) for part in split3(rows))
    for v, ref in enumerate(own_refs):
        ref[...] = own[v : v + 1]


def finish(core, col, wide, other):
    shapes = [(48, 192), (48, DIM), (6, 128), (48, DIM)] + [(1, 48)] * 6
    return pl.pallas_call(
        finish_kernel,
        out_shape=[pltpu.HBM(shape, F32) for shape in shapes],
        in_specs=[SMEM] * 2 + [VMEM] * 2,
        out_specs=[VMEM] * len(shapes),
        compiler_params=params("finish"),
        cost_estimate=cost(1),
        name="finish",
    )(core, col, wide, other)


def joint_kernel(core_ref, last_ref, other_ref, joint_ref, joint_bias_ref):
    last = join(core_ref, last_ref, other_ref)
    chunks = [last[48 * i : 48 * (i + 1)] for i in range(5)]
    heads = [chunks[0][:, 0:64], chunks[0][:, 64:128], chunks[1][:, 0:64]]
    joint_ref[...] = jnp.concatenate([v for h in range(3) for v in (heads[h], chunks[2 + h])], axis=1)
    sums = last[240:248] + last[248:256]
    heads = [sums[0:1, 0:64], sums[0:1, 64:128], sums[1:2, 0:64]]
    joint_bias_ref[...] = jnp.concatenate(
        [jnp.concatenate([heads[h], sums[2 + h : 3 + h, 64:128]], axis=1) for h in range(3)], axis=0
    )


def joint_gradient(core, last, other):
    return pl.pallas_call(
        joint_kernel,
        out_shape=[pltpu.HBM(shape, F32) for shape in ((48, 576), (3, 128))],
        in_specs=[SMEM] + [VMEM] * 2,
        out_specs=[VMEM] * 2,
        compiler_params=params("joint_gradient"),
        cost_estimate=cost(1),
        name="joint_gradient",
    )(core, last, other)


def exchange(blocks, axis):
    return lax.all_to_all(blocks, axis, 0, 0, tiled=True)


def around(v, axis, shift):
    return lax.ppermute(v, axis, [(i, (i + shift) % 4) for i in range(4)])


def swap_cores(v):
    return lax.ppermute(v, "dp", [(0, 1), (1, 0)])


def per_device(
    inputs,
    segments,
    joint_weight,
    joint_bias,
    output_weight,
    output_bias,
    first_norm_gain,
    shift_first,
    up_weight,
    up_bias,
    down_weight,
    down_bias,
    second_norm_gain,
    second_norm_shift,
    cotangent,
):
    core = lax.axis_index("dp")
    col = lax.axis_index(COL)
    row = lax.axis_index("row")
    my_z, my_y = lax.axis_index("z"), lax.axis_index("y")
    core_word = core.reshape(1).astype(jnp.int32)
    row_word = row.reshape(1).astype(jnp.int32)

    def by_col(a):
        return jnp.transpose(a.reshape(48, NCOL, TOK), (1, 0, 2))

    blocks = by_col(inputs)
    blocks, up_weight, down_weight, output_weight = lax.optimization_barrier(
        (blocks, up_weight, down_weight, output_weight)
    )
    x_t = exchange(blocks, COL)
    vectors = jnp.stack(
        [output_bias, first_norm_gain, shift_first, down_bias, second_norm_gain, second_norm_shift], axis=1
    )
    vectors = jnp.pad(jnp.concatenate(split3(vectors), axis=1), ((0, 0), (0, 46)))
    jw = joint_weight.reshape(48, 3, 3, HDIM)
    jw = jnp.concatenate([jw[:, :, 0].reshape(48, 192), vectors, jw[:, :, 1:].reshape(48, 384)], axis=1)
    jw = jnp.broadcast_to(jw[None], (NCOL, 48, JW))
    x_t, jw = lax.optimization_barrier((x_t, jw))
    wj = exchange(jw, COL)
    x4 = lax.all_gather(x_t.reshape(DIM, TOK), "row", axis=0, tiled=False)

    turned = lax.dynamic_slice_in_dim(output_weight, core * 96, 96, 0).T
    my_bias = lax.dynamic_slice_in_dim(up_bias, (core * NCOL + col) * 24, 24, 0)
    my_bias = jnp.pad(jnp.stack(split3(my_bias)), ((0, 45), (0, 8)))
    turned = jnp.concatenate([turned, my_bias], axis=1).reshape(3, 16, 128)
    turned = jnp.transpose(turned, (1, 0, 2)).reshape(16, 384)
    shard = jnp.concatenate(
        [
            lax.dynamic_slice_in_dim(up_weight, core * 384, 384, 1),
            lax.dynamic_slice_in_dim(down_weight, core * 384, 384, 1),
            turned,
        ],
        axis=0,
    )
    shard = lax.optimization_barrier((shard, x_t))[0]
    everything = lax.all_gather(shard, ("dp", "row", "z", "y"), axis=0, tiled=False)
    everything = everything.reshape(2, NROW, NCOL, 112, 384)
    up_b = jnp.sum(everything[:, :, :, 96:99, 96:120].astype(F32), axis=3)
    up_b = jnp.transpose(up_b, (1, 0, 2, 3)).reshape(NROW, DIM)

    bias3 = joint_bias.reshape(3, 2, HDIM)
    bias = jnp.concatenate(
        [
            bias3[:, 0].reshape(192),
            jnp.zeros((64,), F32),
            jnp.concatenate([jnp.zeros((3, HDIM), F32), bias3[:, 1]], axis=1).reshape(384),
        ]
    ).reshape(1, JW)
    seg = segments.reshape(SLOTS, TOK)
    shift = lax.rem(TOK - lax.rem(col, PER_HEAD) * SHARE, TOK).reshape(1).astype(jnp.int32)

    arrived = exchange(project(x4, wj, bias, by_col(cotangent)), COL)
    qa, o, o_blocks = attend(shift, arrived, seg)

    att = exchange(o_blocks, ALL)
    same, sent, d_blocks, fin, dh1 = tokenwise(row_word, att, x_t, arrived, wj, up_b, everything)

    d_blocks, same, sent = lax.optimization_barrier((d_blocks, same, sent))
    pieces = [jnp.concatenate([same, sent[d]], axis=0) for d in range(NROW)]
    grad_o = exchange(d_blocks, ALL)
    got = [around(pieces[d], "row", d) for d in range(1, NROW)]
    grad_o, own_piece = lax.optimization_barrier((grad_o, pieces[0]))
    back_a, doa, turned_qd, acc = attend_back_first(arrived, grad_o, qa, o, fin, seg)
    back_b = attend_back_second(qa, doa, turned_qd, acc, arrived, seg)
    back_a = exchange(back_a, COL)
    back_b, got, own_piece, back_a = lax.optimization_barrier((back_b, got, own_piece, back_a))
    got = [own_piece, *got]
    theirs = [swap_cores(v) for v in got]
    wide = weight_grads(core_word, got, theirs).reshape(4, 4, WROWS // 2, 128)
    back_b, back_a = lax.optimization_barrier((back_b, back_a))
    back_b = exchange(back_b, COL)
    near = [lax.dynamic_index_in_dim(wide, lax.rem(my_z + d, 4), 0, keepdims=False) for d in range(4)]
    near = [near[0]] + [around(near[d], "z", d) for d in range(1, 4)]
    wide = near[0].astype(F32) + near[1].astype(F32) + near[2].astype(F32) + near[3].astype(F32)
    wide = wide.astype(BF)

    din, mine_j, other_j, layer_output = project_back(core_word, back_a, back_b, wj, x4)
    theirs_j = swap_cores(other_j)
    din = exchange(din, "row")
    near = [lax.dynamic_index_in_dim(wide, lax.rem(my_y + d, 4), 0, keepdims=False) for d in range(4)]
    din, near = lax.optimization_barrier((din, near))
    near = [near[0]] + [around(near[d], "y", d) for d in range(1, 4)]
    mixed = exchange(last_payload(mine_j, theirs_j, din, dh1), COL)
    wide = near[0].astype(F32) + near[1].astype(F32) + near[2].astype(F32) + near[3].astype(F32)
    grad_out, grad_up, grad_up_bias, grad_down, *own = finish(
        core_word, col.reshape(1).astype(jnp.int32), wide, swap_cores(wide)
    )
    last = jnp.sum(mixed[:, :128].astype(F32), axis=0)
    grad_inputs = jnp.transpose(mixed[:, 128:].astype(F32), (1, 0, 2)).reshape(48, 2048)
    grad_joint, grad_joint_bias = joint_gradient(core_word, last, swap_cores(last))
    own = [v.reshape(48) for v in own]

    return (
        layer_output,
        grad_inputs,
        grad_joint,
        grad_joint_bias.reshape(384),
        grad_out.T,
        own[5],
        own[0],
        own[1],
        grad_up,
        grad_up_bias.reshape(768),
        grad_down,
        own[4],
        own[2],
        own[3],
    )


def solution(mesh):
    sizes = (mesh.shape["dp"], mesh.shape["row"], 4, 4)
    fine = jax.sharding.Mesh(mesh.devices.reshape(sizes), ("dp", "row", "z", "y"))
    grid = P(COL, ("dp", "row"))
    block = P(COL, "row")
    return jax.shard_map(
        per_device,
        mesh=fine,
        in_specs=(
            grid, P("dp", None), block, P("row"), P("row", COL), P(COL), P(COL), P(COL),
            block, P("row"), block, P(COL), P(COL), P(COL), grid,
        ),
        out_specs=(
            grid, grid, block, P("row"), P("row", COL), P(COL), P(COL), P(COL),
            block, P("row"), block, P(COL), P(COL), P(COL),
        ),
        check_vma=False,
    )
```

profile of v0, /device:TPU:1, one launch (start us, length us, event | category | flops | bytes accessed | tf_op | source)
XLA Modules:
  0.0 288.8 jit_solution(9480187543451676752)
XLA Ops:
  8.9 8.6 %all-to-all-start = ((bf16[16,48,128]{2,1,0:T(8,128)(2,1)}), bf16[16,48,128]{2,1,0:T(8,128)(2,1)S(1)}, u32[]{:S(2)}, u32[]{:S(2)}) async-start(bf16[16,48,128]{2,1,0:T(8,128)(2,1)} %bitcast_bitcast_fusion.1), calls=%async_computation | async-start | bytes 393216 | tf_op jit(solution)/shard_map/all_to_all | solution.py:782
  25.8 5.2 %all-to-all-start.1 = ((bf16[16,48,640]{2,1,0:T(8,128)(2,1)}), bf16[16,48,640]{2,1,0:T(8,128)(2,1)S(1)}, u32[]{:S(2)}, u32[]{:S(2)}) async-start(bf16[16,48,640]{2,1,0:T(8,128)(2,1)} %broadcast_in_dim.4), calls=%async_computation.1 | async-start | bytes 1966080 | tf_op jit(solution)/shard_map/all_to_all | solution.py:782
  31.4 12.7 %all_gather.9.x_ref = bf16[4,768,128]{2,1,0:T(8,128)(2,1)S(1)} all-gather(bf16[1,768,128]{2,1,0:T(8,128)(2,1)S(1)} %bitcast.95), channel_id=1, replica_groups=mesh['dp'=2,'row'=4,'z'=4,'y'=4] {'row'}, dimensions={0}, use_global_device_ids=true | all-gather | bytes 983040 | tf_op jit(solution)/shard_map/all_gather | solution.py:834
  46.1 2.5 project.1
  48.6 5.2 %all-to-all-start.2 = ((bf16[16,624,128]{2,1,0:T(8,128)(2,1)}), bf16[16,624,128]{2,1,0:T(8,128)(2,1)S(1)}, u32[]{:S(2)}, u32[]{:S(2)}) async-start(bf16[16,624,128]{2,1,0:T(8,128)(2,1)} %project.1), calls=%async_computation.2 | async-start | bytes 5111808 | tf_op jit(solution)/shard_map/all_to_all | solution.py:782
  53.8 34.1 %all-to-all-done.2.q_ref.kv_ref.cot_ref = bf16[16,624,128]{2,1,0:T(8,128)(2,1)S(1)} async-done(((bf16[16,624,128]{2,1,0:T(8,128)(2,1)}), bf16[16,624,128]{2,1,0:T(8,128)(2,1)S(1)}, u32[]{:S(2)}, u32[]{:S(2)}) %all-to-all-start.2) | async-done | bytes 2555936 | tf_op jit(solution)/shard_map/all_to_all | solution.py:782
  87.9 19.9 %attend.1 = (bf16[1664,144]{1,0:T(8,128)(2,1)}, f32[1664,64]{1,0:T(8,128)}, bf16[64,16,128]{2,1,0:T(8,128)(2,1)}) custom-call(s32[1]{0:T(128)} %bitcast.1.shift_ref, bf16[16,624,128]{2,1,0:T(8,128)(2,1)S(1)} %all-to-all-done.2.q_ref.kv_ref.cot_ref, bf16[16,624,128]{2,1,0:T(8,128)(2,1)S(1)} %all-to-all-done.2.q_ref.kv_ref.cot_ref, s32[64,128]{1,0:T(8,128)S(1)} %bitcast.92), custom_call_target="tpu_custom_call" | custom-call | flops 20000000000 | bytes 40000000 | tf_op jit(solution)/shard_map/attend/pallas_call | solution.py:212
  107.8 12.5 %all-to-all-start.3 = ((bf16[64,16,128]{2,1,0:T(8,128)(2,1)}), bf16[64,16,128]{2,1,0:T(8,128)(2,1)}, u32[]{:S(2)}, u32[]{:S(2)}) async-start(bf16[64,16,128]{2,1,0:T(8,128)(2,1)} %get-tuple-element.71), calls=%async_computation.3 | async-start | bytes 524288 | tf_op jit(solution)/shard_map/all_to_all | solution.py:782
  122.2 7.0 %all-to-all-done.3.att_ref = bf16[64,16,128]{2,1,0:T(8,128)(2,1)} async-done(((bf16[64,16,128]{2,1,0:T(8,128)(2,1)}), bf16[64,16,128]{2,1,0:T(8,128)(2,1)}, u32[]{:S(2)}, u32[]{:S(2)}) %all-to-all-start.3) | async-done | bytes 262176 | tf_op jit(solution)/shard_map/all_to_all | solution.py:782
  129.3 12.3 %tokenwise.1 = (bf16[2352,128]{1,0:T(8,128)(2,1)}, bf16[4,1728,128]{2,1,0:T(8,128)(2,1)}, bf16[64,16,128]{2,1,0:T(8,128)(2,1)}, bf16[16,48,128]{2,1,0:T(8,128)(2,1)}, f32[768,128]{1,0:T(8,128)}) custom-call(s32[1]{0:T(128)} %bitcast.13.row_ref, bf16[64,16,128]{2,1,0:T(8,128)(2,1)} %all-to-all-done.3.att_ref, bf16[16,48,128]{2,1,0:T(8,128)(2,1)} %copy-done.7, ...), custom_call_target="tpu_custom_call" | custom-call | flops 15000000512 | bytes 30000000 | tf_op jit(solution)/shard_map/tokenwise/pallas_call | solution.py:512
  143.2 5.5 %all-to-all-start.4 = ((bf16[64,16,128]{2,1,0:T(8,128)(2,1)}), bf16[64,16,128]{2,1,0:T(8,128)(2,1)}, u32[]{:S(2)}, u32[]{:S(2)}) async-start(bf16[64,16,128]{2,1,0:T(8,128)(2,1)} %get-tuple-element.79), calls=%async_computation.4 | async-start | bytes 524288 | tf_op jit(solution)/shard_map/all_to_all | solution.py:782
  148.7 2.4 pad_maximum_fusion
  152.1 2.6 collective-permute-start.1
  155.8 2.1 all-to-all-done.4.do_ref
  157.9 20.6 %attend_back_first.1 = (bf16[16,304,128]{2,1,0:T(8,128)(2,1)}, bf16[1664,80]{1,0:T(8,128)(2,1)}, bf16[128,1664]{1,0:T(8,128)(2,1)}, f32[1664,128]{1,0:T(8,128)}) custom-call(bf16[16,624,128]{2,1,0:T(8,128)(2,1)} %copy-done.1, bf16[64,16,128]{2,1,0:T(8,128)(2,1)} %all-to-all-done.4.do_ref, bf16[1664,144]{1,0:T(8,128)(2,1)} %get-tuple-element.70.qa_ref, ...), custom_call_target="tpu_custom_call" | custom-call | flops 17999998976 | bytes 36000000 | tf_op jit(solution)/shard_map/attend_back_first/pallas_call | solution.py:308
  178.4 4.5 %all-to-all-start.5 = ((bf16[16,304,128]{2,1,0:T(8,128)(2,1)}), bf16[16,304,128]{2,1,0:T(8,128)(2,1)}, u32[]{:S(2)}, u32[]{:S(2)}) async-start(bf16[16,304,128]{2,1,0:T(8,128)(2,1)} %get-tuple-element.89), calls=%async_computation.5 | async-start | bytes 2490368 | tf_op jit(solution)/shard_map/all_to_all | solution.py:782
  183.0 19.6 %attend_back_second.1 = bf16[16,320,128]{2,1,0:T(8,128)(2,1)} custom-call(bf16[1664,144]{1,0:T(8,128)(2,1)} %get-tuple-element.70.qa_ref, bf16[1664,80]{1,0:T(8,128)(2,1)} %get-tuple-element.85.doa_ref, bf16[128,1664]{1,0:T(8,128)(2,1)} %get-tuple-element.86.turned_ref, f32[1664,128]{1,0:T(8,128)} %get-tuple-element.87.acc_in, ...), custom_call_target="tpu_custom_call" | custom-call | flops 17999998976 | bytes 36000000 | tf_op jit(solution)/shard_map/attend_back_second/pallas_call | solution.py:340
  202.5 3.8 %collective-permute-start.4 = (bf16[4080,128]{1,0:T(8,128)(2,1)}, bf16[4080,128]{1,0:T(8,128)(2,1)}, u32[]{:S(2)}, u32[]{:S(2)}) collective-permute-start(bf16[4080,128]{1,0:T(8,128)(2,1)} %get-tuple-element.98.refs_0_), channel_id=1, source_target_pairs={{0,64},{64,0},{1,65},{65,1},{2,66},{66,2},{3,67},{67,3},{4,68},{68... | collective-permute-start | bytes 3133448 | tf_op jit(solution)/shard_map/ppermute | solution.py:790
  206.9 6.9 %all-to-all-start.6 = ((bf16[16,320,128]{2,1,0:T(8,128)(2,1)}), bf16[16,320,128]{2,1,0:T(8,128)(2,1)}, u32[]{:S(2)}, u32[]{:S(2)}) async-start(bf16[16,320,128]{2,1,0:T(8,128)(2,1)} %attend_back_second.1), calls=%async_computation.6 | async-start | bytes 2621440 | tf_op jit(solution)/shard_map/all_to_all | solution.py:782
  213.9 6.9 %weight_grads.1 = bf16[16,384,128]{2,1,0:T(8,128)(2,1)} custom-call(s32[1]{0:T(128)} %bitcast.core_ref, bf16[4080,128]{1,0:T(8,128)(2,1)} %get-tuple-element.98.refs_0_, bf16[4080,128]{1,0:T(8,128)(2,1)} %collective-permute-done.refs_1_, bf16[4080,128]{1,0:T(8,128)(2,1)} %collective-permute-done.1.refs_2_, bf16[4080,128]{1,0:T(8,128)(2,1)} %collective-permute-done.2.refs_3_, ...), custom_call_target="tpu_custom_call" | custom-call | flops 1000000000 | bytes 2000000 | tf_op jit(solution)/shard_map/weight_grads/pallas_call | solution.py:608
  220.8 2.3 dynamic-slice_bitcast_fusion.2
  223.1 2.5 collective-permute-start.10
  227.3 6.5 %all-to-all-done.6.second_ref = bf16[16,320,128]{2,1,0:T(8,128)(2,1)} async-done(((bf16[16,320,128]{2,1,0:T(8,128)(2,1)}), bf16[16,320,128]{2,1,0:T(8,128)(2,1)}, u32[]{:S(2)}, u32[]{:S(2)}) %all-to-all-start.6) | async-done | bytes 1310752 | tf_op jit(solution)/shard_map/all_to_all | solution.py:782
  233.8 6.2 %project_back.1 = (bf16[4,768,128]{2,1,0:T(8,128)(2,1)}, bf16[16,128,128]{2,1,0:T(8,128)(2,1)}, bf16[16,128,128]{2,1,0:T(8,128)(2,1)}, bf16[48,2048]{1,0:T(8,128)(2,1)}) custom-call(s32[1]{0:T(128)} %bitcast.core_ref, bf16[16,304,128]{2,1,0:T(8,128)(2,1)} %all-to-all-done.5.first_ref, bf16[16,320,128]{2,1,0:T(8,128)(2,1)} %all-to-all-done.6.second_ref, ...), custom_call_target="tpu_custom_call" | custom-call | flops 5000000000 | bytes 10000000 | tf_op jit(solution)/shard_map/project_back/pallas_call | solution.py:678
  240.1 3.6 %all-to-all-start.7 = ((bf16[4,768,128]{2,1,0:T(8,128)(2,1)}), bf16[4,768,128]{2,1,0:T(8,128)(2,1)S(1)}, u32[]{:S(2)}, u32[]{:S(2)}) async-start(bf16[4,768,128]{2,1,0:T(8,128)(2,1)} %get-tuple-element.97), calls=%async_computation.7 | async-start | bytes 1572864 | tf_op jit(solution)/shard_map/all_to_all | solution.py:782
  243.7 2.4 collective-permute-start.3
  246.1 3.2 %collective-permute-done.9 = bf16[4,384,128]{2,1,0:T(8,128)(2,1)} collective-permute-done((bf16[4,384,128]{2,1,0:T(8,128)(2,1)}, bf16[4,384,128]{2,1,0:T(8,128)(2,1)}, u32[]{:S(2)}, u32[]{:S(2)}) %collective-permute-start.9) | collective-permute-done | bytes 393248 | tf_op jit(solution)/shard_map/ppermute | solution.py:786
  250.9 2.4 all-to-all-done.7.din_ref
  254.5 6.6 %all-to-all-start.8 = ((bf16[16,176,128]{2,1,0:T(8,128)(2,1)}), bf16[16,176,128]{2,1,0:T(8,128)(2,1)S(1)}, u32[]{:S(2)}, u32[]{:S(2)}) async-start(bf16[16,176,128]{2,1,0:T(8,128)(2,1)} %last_payload.1), calls=%async_computation.8 | async-start | bytes 1441792 | tf_op jit(solution)/shard_map/all_to_all | solution.py:782
  262.4 2.4 collective-permute-start.13
  266.0 8.2 %collective-permute-done.12 = bf16[384,128]{1,0:T(8,128)(2,1)S(1)} collective-permute-done((bf16[384,128]{1,0:T(8,128)(2,1)S(1)}, bf16[384,128]{1,0:T(8,128)(2,1)S(1)}, u32[]{:S(2)}, u32[]{:S(2)}) %collective-permute-start.12) | collective-permute-done | bytes 98336 | tf_op jit(solution)/shard_map/ppermute | solution.py:786
  275.0 2.9 %collective-permute-start.15 = (f32[384,128]{1,0:T(8,128)S(1)}, f32[384,128]{1,0:T(8,128)S(1)}, u32[]{:S(2)}, u32[]{:S(2)}) collective-permute-start(f32[384,128]{1,0:T(8,128)S(1)} %convert_add_fusion.1.wide_ref), channel_id=1, source_target_pairs={{0,64},{64,0},{1,65},{65,1},{2,66},{66,2},{3,67},{67,3},{4,68},{68... | collective-permute-start | bytes 589832 | tf_op jit(solution)/shard_map/ppermute | solution.py:790
  (95 shorter events, 30.3 us)
Async XLA Ops:
  7.2 18.5 %copy-start.10 = (f32[384]{0:T(512)S(1)}, f32[384]{0:T(512)}, u32[]{:S(2)}) copy-start(f32[384]{0:T(512)} %param.18) | copy-start | bytes 4612
  8.9 15.8 %all-to-all-start = ((bf16[16,48,128]{2,1,0:T(8,128)(2,1)}), bf16[16,48,128]{2,1,0:T(8,128)(2,1)S(1)}, u32[]{:S(2)}, u32[]{:S(2)}) async-start(bf16[16,48,128]{2,1,0:T(8,128)(2,1)} %bitcast_bitcast_fusion.1), calls=%async_computation | async-start | bytes 393216 | tf_op jit(solution)/shard_map/all_to_all | solution.py:782
  17.5 102.8 %all-gather.3.cloned.1.call-start = ((), (), s32[]{:S(2)}) async-start(), calls=%async_computation.9 | async-start | bytes 11096064 | tf_op jit(solution)/shard_map/all_gather | solution.py:850
  24.7 19.5 %copy-start.7 = (bf16[16,48,128]{2,1,0:T(8,128)(2,1)}, bf16[16,48,128]{2,1,0:T(8,128)(2,1)S(1)}, u32[]{:S(2)}) copy-start(bf16[16,48,128]{2,1,0:T(8,128)(2,1)S(1)} %all-to-all-done.x_ref) | copy-start | bytes 589828
  25.8 20.2 %all-to-all-start.1 = ((bf16[16,48,640]{2,1,0:T(8,128)(2,1)}), bf16[16,48,640]{2,1,0:T(8,128)(2,1)S(1)}, u32[]{:S(2)}, u32[]{:S(2)}) async-start(bf16[16,48,640]{2,1,0:T(8,128)(2,1)} %broadcast_in_dim.4), calls=%async_computation.1 | async-start | bytes 1966080 | tf_op jit(solution)/shard_map/all_to_all | solution.py:782
  48.6 39.3 %copy-start.4 = (s32[1,8192]{1,0:T(1,128)S(1)}, s32[1,8192]{1,0:T(1,128)}, u32[]{:S(2)}) copy-start(s32[1,8192]{1,0:T(1,128)} %param.16) | copy-start | bytes 98308
  48.6 39.3 %all-to-all-start.2 = ((bf16[16,624,128]{2,1,0:T(8,128)(2,1)}), bf16[16,624,128]{2,1,0:T(8,128)(2,1)S(1)}, u32[]{:S(2)}, u32[]{:S(2)}) async-start(bf16[16,624,128]{2,1,0:T(8,128)(2,1)} %project.1), calls=%async_computation.2 | async-start | bytes 5111808 | tf_op jit(solution)/shard_map/all_to_all | solution.py:782
  87.9 19.9 %copy-start.1 = (bf16[16,624,128]{2,1,0:T(8,128)(2,1)}, bf16[16,624,128]{2,1,0:T(8,128)(2,1)S(1)}, u32[]{:S(2)}) copy-start(bf16[16,624,128]{2,1,0:T(8,128)(2,1)S(1)} %all-to-all-done.2.q_ref.kv_ref.cot_ref) | copy-start | bytes 7667716
  107.8 21.5 %all-to-all-start.3 = ((bf16[64,16,128]{2,1,0:T(8,128)(2,1)}), bf16[64,16,128]{2,1,0:T(8,128)(2,1)}, u32[]{:S(2)}, u32[]{:S(2)}) async-start(bf16[64,16,128]{2,1,0:T(8,128)(2,1)} %get-tuple-element.71), calls=%async_computation.3 | async-start | bytes 524288 | tf_op jit(solution)/shard_map/all_to_all | solution.py:782
  143.2 14.6 %all-to-all-start.4 = ((bf16[64,16,128]{2,1,0:T(8,128)(2,1)}), bf16[64,16,128]{2,1,0:T(8,128)(2,1)}, u32[]{:S(2)}, u32[]{:S(2)}) async-start(bf16[64,16,128]{2,1,0:T(8,128)(2,1)} %get-tuple-element.79), calls=%async_computation.4 | async-start | bytes 524288 | tf_op jit(solution)/shard_map/all_to_all | solution.py:782
  151.2 51.4 %collective-permute-start = (bf16[4080,128]{1,0:T(8,128)(2,1)}, bf16[4080,128]{1,0:T(8,128)(2,1)}, u32[]{:S(2)}, u32[]{:S(2)}) collective-permute-start(bf16[4080,128]{1,0:T(8,128)(2,1)} %get-tuple-element.128), channel_id=1, source_target_pairs={{0,16},{16,32},{32,48},{48,0},{1,17},{17,33},{33,49},{49,1},{2,18}... | collective-permute-start | bytes 3133448 | tf_op jit(solution)/shard_map/ppermute | solution.py:786
  152.1 50.4 %collective-permute-start.1 = (bf16[4080,128]{1,0:T(8,128)(2,1)}, bf16[4080,128]{1,0:T(8,128)(2,1)}, u32[]{:S(2)}, u32[]{:S(2)}) collective-permute-start(bf16[4080,128]{1,0:T(8,128)(2,1)} %get-tuple-element.129), channel_id=1, source_target_pairs={{0,32},{16,48},{32,0},{48,16},{1,33},{17,49},{33,1},{49,17},{2,34}... | collective-permute-start | bytes 3133448 | tf_op jit(solution)/shard_map/ppermute | solution.py:786
  154.7 47.8 %collective-permute-start.2 = (bf16[4080,128]{1,0:T(8,128)(2,1)}, bf16[4080,128]{1,0:T(8,128)(2,1)}, u32[]{:S(2)}, u32[]{:S(2)}) collective-permute-start(bf16[4080,128]{1,0:T(8,128)(2,1)} %get-tuple-element.127), channel_id=1, source_target_pairs={{0,48},{16,0},{32,16},{48,32},{1,49},{17,1},{33,17},{49,33},{2,50}... | collective-permute-start | bytes 3133448 | tf_op jit(solution)/shard_map/ppermute | solution.py:786
  178.4 24.1 %all-to-all-start.5 = ((bf16[16,304,128]{2,1,0:T(8,128)(2,1)}), bf16[16,304,128]{2,1,0:T(8,128)(2,1)}, u32[]{:S(2)}, u32[]{:S(2)}) async-start(bf16[16,304,128]{2,1,0:T(8,128)(2,1)} %get-tuple-element.89), calls=%async_computation.5 | async-start | bytes 2490368 | tf_op jit(solution)/shard_map/all_to_all | solution.py:782
  202.5 11.3 %collective-permute-start.4 = (bf16[4080,128]{1,0:T(8,128)(2,1)}, bf16[4080,128]{1,0:T(8,128)(2,1)}, u32[]{:S(2)}, u32[]{:S(2)}) collective-permute-start(bf16[4080,128]{1,0:T(8,128)(2,1)} %get-tuple-element.98.refs_0_), channel_id=1, source_target_pairs={{0,64},{64,0},{1,65},{65,1},{2,66},{66,2},{3,67},{67,3},{4,68},{68... | collective-permute-start | bytes 3133448 | tf_op jit(solution)/shard_map/ppermute | solution.py:790
  206.3 7.5 %collective-permute-start.5 = (bf16[4080,128]{1,0:T(8,128)(2,1)}, bf16[4080,128]{1,0:T(8,128)(2,1)}, u32[]{:S(2)}, u32[]{:S(2)}) collective-permute-start(bf16[4080,128]{1,0:T(8,128)(2,1)} %collective-permute-done.refs_1_), channel_id=1, source_target_pairs={{0,64},{64,0},{1,65},{65,1},{2,66},{66,2},{3,67},{67,3},{4,68},{68... | collective-permute-start | bytes 3133448 | tf_op jit(solution)/shard_map/ppermute | solution.py:790
  206.4 7.4 %collective-permute-start.6 = (bf16[4080,128]{1,0:T(8,128)(2,1)}, bf16[4080,128]{1,0:T(8,128)(2,1)}, u32[]{:S(2)}, u32[]{:S(2)}) collective-permute-start(bf16[4080,128]{1,0:T(8,128)(2,1)} %collective-permute-done.1.refs_2_), channel_id=1, source_target_pairs={{0,64},{64,0},{1,65},{65,1},{2,66},{66,2},{3,67},{67,3},{4,68},{68... | collective-permute-start | bytes 3133448 | tf_op jit(solution)/shard_map/ppermute | solution.py:790
  206.9 7.0 %collective-permute-start.7 = (bf16[4080,128]{1,0:T(8,128)(2,1)}, bf16[4080,128]{1,0:T(8,128)(2,1)}, u32[]{:S(2)}, u32[]{:S(2)}) collective-permute-start(bf16[4080,128]{1,0:T(8,128)(2,1)} %collective-permute-done.2.refs_3_), channel_id=1, source_target_pairs={{0,64},{64,0},{1,65},{65,1},{2,66},{66,2},{3,67},{67,3},{4,68},{68... | collective-permute-start | bytes 3133448 | tf_op jit(solution)/shard_map/ppermute | solution.py:790
  206.9 26.9 %all-to-all-start.6 = ((bf16[16,320,128]{2,1,0:T(8,128)(2,1)}), bf16[16,320,128]{2,1,0:T(8,128)(2,1)}, u32[]{:S(2)}, u32[]{:S(2)}) async-start(bf16[16,320,128]{2,1,0:T(8,128)(2,1)} %attend_back_second.1), calls=%async_computation.6 | async-start | bytes 2621440 | tf_op jit(solution)/shard_map/all_to_all | solution.py:782
  223.1 23.0 %collective-permute-start.10 = (bf16[4,384,128]{2,1,0:T(8,128)(2,1)}, bf16[4,384,128]{2,1,0:T(8,128)(2,1)}, u32[]{:S(2)}, u32[]{:S(2)}) collective-permute-start(bf16[4,384,128]{2,1,0:T(8,128)(2,1)} %get-tuple-element.125), channel_id=1, source_target_pairs={{0,12},{4,0},{8,4},{12,8},{1,13},{5,1},{9,5},{13,9},{2,14},{6,2},{... | collective-permute-start | bytes 1179656 | tf_op jit(solution)/shard_map/ppermute | solution.py:786
  225.6 20.5 %collective-permute-start.8 = (bf16[4,384,128]{2,1,0:T(8,128)(2,1)}, bf16[4,384,128]{2,1,0:T(8,128)(2,1)}, u32[]{:S(2)}, u32[]{:S(2)}) collective-permute-start(bf16[4,384,128]{2,1,0:T(8,128)(2,1)} %get-tuple-element.124), channel_id=1, source_target_pairs={{0,4},{4,8},{8,12},{12,0},{1,5},{5,9},{9,13},{13,1},{2,6},{6,10},{... | collective-permute-start | bytes 1179656 | tf_op jit(solution)/shard_map/ppermute | solution.py:786
  225.6 23.7 %collective-permute-start.9 = (bf16[4,384,128]{2,1,0:T(8,128)(2,1)}, bf16[4,384,128]{2,1,0:T(8,128)(2,1)}, u32[]{:S(2)}, u32[]{:S(2)}) collective-permute-start(bf16[4,384,128]{2,1,0:T(8,128)(2,1)} %get-tuple-element.126), channel_id=1, source_target_pairs={{0,8},{4,12},{8,0},{12,4},{1,9},{5,13},{9,1},{13,5},{2,10},{6,14},... | collective-permute-start | bytes 1179656 | tf_op jit(solution)/shard_map/ppermute | solution.py:786
  240.1 13.3 %copy-start.5 = (bf16[16,128,128]{2,1,0:T(8,128)(2,1)S(1)}, bf16[16,128,128]{2,1,0:T(8,128)(2,1)}, u32[]{:S(2)}) copy-start(bf16[16,128,128]{2,1,0:T(8,128)(2,1)} %get-tuple-element.95.mine_ref) | copy-start | bytes 1572868
  240.1 13.3 %copy-start.6 = (f32[768,128]{1,0:T(8,128)S(1)}, f32[768,128]{1,0:T(8,128)}, u32[]{:S(2)}) copy-start(f32[768,128]{1,0:T(8,128)} %get-tuple-element.103.dh1_ref) | copy-start | bytes 1179652
  240.1 13.3 %all-to-all-start.7 = ((bf16[4,768,128]{2,1,0:T(8,128)(2,1)}), bf16[4,768,128]{2,1,0:T(8,128)(2,1)S(1)}, u32[]{:S(2)}, u32[]{:S(2)}) async-start(bf16[4,768,128]{2,1,0:T(8,128)(2,1)} %get-tuple-element.97), calls=%async_computation.7 | async-start | bytes 1572864 | tf_op jit(solution)/shard_map/all_to_all | solution.py:782
  243.7 9.6 %collective-permute-start.3 = (bf16[16,128,128]{2,1,0:T(8,128)(2,1)}, bf16[16,128,128]{2,1,0:T(8,128)(2,1)S(1)}, u32[]{:S(2)}, u32[]{:S(2)}) collective-permute-start(bf16[16,128,128]{2,1,0:T(8,128)(2,1)} %get-tuple-element.96), channel_id=1, source_target_pairs={{0,64},{64,0},{1,65},{65,1},{2,66},{66,2},{3,67},{67,3},{4,68},{68... | collective-permute-start | bytes 1572872 | tf_op jit(solution)/shard_map/ppermute | solution.py:790
  254.5 25.4 %all-to-all-start.8 = ((bf16[16,176,128]{2,1,0:T(8,128)(2,1)}), bf16[16,176,128]{2,1,0:T(8,128)(2,1)S(1)}, u32[]{:S(2)}, u32[]{:S(2)}) async-start(bf16[16,176,128]{2,1,0:T(8,128)(2,1)} %last_payload.1), calls=%async_computation.8 | async-start | bytes 1441792 | tf_op jit(solution)/shard_map/all_to_all | solution.py:782
  261.0 13.1 %collective-permute-start.12 = (bf16[384,128]{1,0:T(8,128)(2,1)S(1)}, bf16[384,128]{1,0:T(8,128)(2,1)S(1)}, u32[]{:S(2)}, u32[]{:S(2)}) collective-permute-start(bf16[384,128]{1,0:T(8,128)(2,1)S(1)} %get-tuple-element.107), channel_id=1, source_target_pairs={{0,1},{1,2},{2,3},{3,0},{4,5},{5,6},{6,7},{7,4},{8,9},{9,10},{10,1... | collective-permute-start | bytes 294920 | tf_op jit(solution)/shard_map/ppermute | solution.py:786
  262.4 12.5 %collective-permute-start.13 = (bf16[384,128]{1,0:T(8,128)(2,1)S(1)}, bf16[384,128]{1,0:T(8,128)(2,1)S(1)}, u32[]{:S(2)}, u32[]{:S(2)}) collective-permute-start(bf16[384,128]{1,0:T(8,128)(2,1)S(1)} %get-tuple-element.108), channel_id=1, source_target_pairs={{0,2},{1,3},{2,0},{3,1},{4,6},{5,7},{6,4},{7,5},{8,10},{9,11},{10,... | collective-permute-start | bytes 294920 | tf_op jit(solution)/shard_map/ppermute | solution.py:786
  264.8 10.1 %collective-permute-start.14 = (bf16[384,128]{1,0:T(8,128)(2,1)S(1)}, bf16[384,128]{1,0:T(8,128)(2,1)S(1)}, u32[]{:S(2)}, u32[]{:S(2)}) collective-permute-start(bf16[384,128]{1,0:T(8,128)(2,1)S(1)} %get-tuple-element.109), channel_id=1, source_target_pairs={{0,3},{1,0},{2,1},{3,2},{4,7},{5,4},{6,5},{7,6},{8,11},{9,8},{10,9... | collective-permute-start | bytes 294920 | tf_op jit(solution)/shard_map/ppermute | solution.py:786
  275.0 4.0 %collective-permute-start.15 = (f32[384,128]{1,0:T(8,128)S(1)}, f32[384,128]{1,0:T(8,128)S(1)}, u32[]{:S(2)}, u32[]{:S(2)}) collective-permute-start(f32[384,128]{1,0:T(8,128)S(1)} %convert_add_fusion.1.wide_ref), channel_id=1, source_target_pairs={{0,64},{64,0},{1,65},{65,1},{2,66},{66,2},{3,67},{67,3},{4,68},{68... | collective-permute-start | bytes 589832 | tf_op jit(solution)/shard_map/ppermute | solution.py:790
  279.9 1.4 collective-permute-start.11
  (5 other events, 38.5 us)
Sparse Core Ops, SparseCore 0:
  25.9 94.0 all-gather.2
where the time goes:
time: 290 us; the launch traced here: 289 us
  Pallas kernels  90.8 us (31%)
  starting transfers between devices  82.5 us (28%)
  waiting for transfers between devices  68.9 us (24%)
  between operations  14.4 us (5%)
  blocking collectives  12.7 us (4%)
  local copies, waits for them, and re-layouts  11.6 us (4%)
  other arithmetic  7.76 us (3%)
    all_to_all x9, starting transfers between devices, exchange(): return lax.all_to_all(blocks, axis, 0, 0, tiled=True)  58.5 us
    all_to_all x9, waiting for transfers between devices, exchange(): return lax.all_to_all(blocks, axis, 0, 0, tiled=True)  55.5 us
    pallas_call x1, Pallas kernels, attend_back_first(): pl.pallas_call(back_first_kernel, grid=(BACK_STEPS,), out_shape=(pltpu.HB...  20.6 us
    pallas_call x1, Pallas kernels, attend(): pl.pallas_call(attend_kernel, grid=(NCOL // FWD_C,), out_shape=(pltpu.HBM...  19.9 us
    pallas_call x1, Pallas kernels, attend_back_second(): pl.pallas_call(back_second_kernel, grid=(BACK_STEPS,), out_shape=pltpu.HB...  19.6 us
    ppermute x9, starting transfers between devices, around(): return lax.ppermute(v, axis, [(i, (i + shift) % 4) for i in range(4)])  13.8 us
    all_gather x1, blocking collectives, per_device(): x4 = lax.all_gather(x_t.reshape(DIM, TOK), 'row', axis=0, tiled=False)  12.7 us
    pallas_call x1, Pallas kernels, tokenwise(): pl.pallas_call(tokenwise_kernel, out_shape=(pltpu.HBM((SAME, TOK), BF), p...  12.3 us
  transfers between devices with their start and end apart: 26, of which 12 were waited for; matrix products, arithmetic and copies ran while one was open for 5% of the time, Pallas kernels for 27%

commit v1 on v0

--- a/solution.py
+++ b/solution.py
@@ -870,7 +870,11 @@
     same, sent, d_blocks, fin, dh1 = tokenwise(row_word, att, x_t, arrived, wj, up_b, everything)
 
     d_blocks, same, sent = lax.optimization_barrier((d_blocks, same, sent))
-    pieces = [jnp.concatenate([same, sent[d]], axis=0) for d in range(NROW)]
+    zero = jnp.minimum(row, 0)
+    pieces = [
+        jnp.concatenate([same, lax.dynamic_index_in_dim(sent, zero + d, 0, keepdims=False)], axis=0)
+        for d in range(NROW)
+    ]
     grad_o = exchange(d_blocks, ALL)
     got = [around(pieces[d], "row", d) for d in range(1, NROW)]
     grad_o, own_piece = lax.optimization_barrier((grad_o, pieces[0]))

time: 290 us -> 290 us (level)
  transfers between devices with their start and end apart: 26 -> 26, of which waited for: 12 -> 12; matrix products, arithmetic and copies ran while one was open for 5% -> 6% of each run, Pallas kernels for 27% -> 27%
where the time goes in v1:
time: 290 us; the launch traced here: 289 us
  Pallas kernels  90.9 us (31%)
  starting transfers between devices  84.1 us (29%)
  waiting for transfers between devices  67.4 us (23%)
  between operations  14.4 us (5%)
  blocking collectives  12.7 us (4%)
  local copies, waits for them, and re-layouts  11.6 us (4%)
  other arithmetic  7.76 us (3%)
    all_to_all x9, starting transfers between devices, exchange(): return lax.all_to_all(blocks, axis, 0, 0, tiled=True)  60.2 us
    all_to_all x9, waiting for transfers between devices, exchange(): return lax.all_to_all(blocks, axis, 0, 0, tiled=True)  54 us
    pallas_call x1, Pallas kernels, attend_back_first(): pl.pallas_call(back_first_kernel, grid=(BACK_STEPS,), out_shape=(pltpu.HB...  20.6 us
    pallas_call x1, Pallas kernels, attend(): pl.pallas_call(attend_kernel, grid=(NCOL // FWD_C,), out_shape=(pltpu.HBM...  19.9 us
    pallas_call x1, Pallas kernels, attend_back_second(): pl.pallas_call(back_second_kernel, grid=(BACK_STEPS,), out_shape=pltpu.HB...  19.6 us
    ppermute x9, starting transfers between devices, around(): return lax.ppermute(v, axis, [(i, (i + shift) % 4) for i in range(4)])  13.8 us
    all_gather x1, blocking collectives, per_device(): x4 = lax.all_gather(x_t.reshape(DIM, TOK), 'row', axis=0, tiled=False)  12.7 us
    pallas_call x1, Pallas kernels, tokenwise(): pl.pallas_call(tokenwise_kernel, out_shape=(pltpu.HBM((SAME, TOK), BF), p...  12.3 us
  transfers between devices with their start and end apart: 26, of which 12 were waited for; matrix products, arithmetic and copies ran while one was open for 6% of the time, Pallas kernels for 27%

profile of v1, /device:TPU:1, one launch (start us, length us, event | category | flops | bytes accessed | tf_op | source)
XLA Modules:
  0.0 288.9 jit_solution(15331464387025967886)
XLA Ops:
  8.9 8.6 %all-to-all-start = ((bf16[16,48,128]{2,1,0:T(8,128)(2,1)}), bf16[16,48,128]{2,1,0:T(8,128)(2,1)S(1)}, u32[]{:S(2)}, u32[]{:S(2)}) async-start(bf16[16,48,128]{2,1,0:T(8,128)(2,1)} %bitcast_bitcast_fusion.1), calls=%async_computation | async-start | bytes 393216 | tf_op jit(solution)/shard_map/all_to_all | solution.py:782
  25.8 5.2 %all-to-all-start.1 = ((bf16[16,48,640]{2,1,0:T(8,128)(2,1)}), bf16[16,48,640]{2,1,0:T(8,128)(2,1)S(1)}, u32[]{:S(2)}, u32[]{:S(2)}) async-start(bf16[16,48,640]{2,1,0:T(8,128)(2,1)} %broadcast_in_dim.4), calls=%async_computation.1 | async-start | bytes 1966080 | tf_op jit(solution)/shard_map/all_to_all | solution.py:782
  31.4 12.7 %all_gather.9.x_ref = bf16[4,768,128]{2,1,0:T(8,128)(2,1)S(1)} all-gather(bf16[1,768,128]{2,1,0:T(8,128)(2,1)S(1)} %bitcast.95), channel_id=1, replica_groups=mesh['dp'=2,'row'=4,'z'=4,'y'=4] {'row'}, dimensions={0}, use_global_device_ids=true | all-gather | bytes 983040 | tf_op jit(solution)/shard_map/all_gather | solution.py:834
  44.1 2.0 all-to-all-done.1.w_ref.vec_ref
  46.1 2.5 project.1
  48.6 5.2 %all-to-all-start.2 = ((bf16[16,624,128]{2,1,0:T(8,128)(2,1)}), bf16[16,624,128]{2,1,0:T(8,128)(2,1)S(1)}, u32[]{:S(2)}, u32[]{:S(2)}) async-start(bf16[16,624,128]{2,1,0:T(8,128)(2,1)} %project.1), calls=%async_computation.2 | async-start | bytes 5111808 | tf_op jit(solution)/shard_map/all_to_all | solution.py:782
  53.8 34.1 %all-to-all-done.2.q_ref.kv_ref.cot_ref = bf16[16,624,128]{2,1,0:T(8,128)(2,1)S(1)} async-done(((bf16[16,624,128]{2,1,0:T(8,128)(2,1)}), bf16[16,624,128]{2,1,0:T(8,128)(2,1)S(1)}, u32[]{:S(2)}, u32[]{:S(2)}) %all-to-all-start.2) | async-done | bytes 2555936 | tf_op jit(solution)/shard_map/all_to_all | solution.py:782
  87.9 19.9 %attend.1 = (bf16[1664,144]{1,0:T(8,128)(2,1)}, f32[1664,64]{1,0:T(8,128)}, bf16[64,16,128]{2,1,0:T(8,128)(2,1)}) custom-call(s32[1]{0:T(128)} %bitcast.1.shift_ref, bf16[16,624,128]{2,1,0:T(8,128)(2,1)S(1)} %all-to-all-done.2.q_ref.kv_ref.cot_ref, bf16[16,624,128]{2,1,0:T(8,128)(2,1)S(1)} %all-to-all-done.2.q_ref.kv_ref.cot_ref, s32[64,128]{1,0:T(8,128)S(1)} %bitcast.92), custom_call_target="tpu_custom_call" | custom-call | flops 20000000000 | bytes 40000000 | tf_op jit(solution)/shard_map/attend/pallas_call | solution.py:212
  107.8 12.5 %all-to-all-start.3 = ((bf16[64,16,128]{2,1,0:T(8,128)(2,1)}), bf16[64,16,128]{2,1,0:T(8,128)(2,1)}, u32[]{:S(2)}, u32[]{:S(2)}) async-start(bf16[64,16,128]{2,1,0:T(8,128)(2,1)} %get-tuple-element.71), calls=%async_computation.3 | async-start | bytes 524288 | tf_op jit(solution)/shard_map/all_to_all | solution.py:782
  122.2 7.0 %all-to-all-done.3.att_ref = bf16[64,16,128]{2,1,0:T(8,128)(2,1)} async-done(((bf16[64,16,128]{2,1,0:T(8,128)(2,1)}), bf16[64,16,128]{2,1,0:T(8,128)(2,1)}, u32[]{:S(2)}, u32[]{:S(2)}) %all-to-all-start.3) | async-done | bytes 262176 | tf_op jit(solution)/shard_map/all_to_all | solution.py:782
  129.3 12.3 %tokenwise.1 = (bf16[2352,128]{1,0:T(8,128)(2,1)}, bf16[4,1728,128]{2,1,0:T(8,128)(2,1)}, bf16[64,16,128]{2,1,0:T(8,128)(2,1)}, bf16[16,48,128]{2,1,0:T(8,128)(2,1)}, f32[768,128]{1,0:T(8,128)}) custom-call(s32[1]{0:T(128)} %bitcast.13.row_ref, bf16[64,16,128]{2,1,0:T(8,128)(2,1)} %all-to-all-done.3.att_ref, bf16[16,48,128]{2,1,0:T(8,128)(2,1)} %copy-done.7, ...), custom_call_target="tpu_custom_call" | custom-call | flops 15000000512 | bytes 30000000 | tf_op jit(solution)/shard_map/tokenwise/pallas_call | solution.py:512
  141.6 5.6 %all-to-all-start.4 = ((bf16[64,16,128]{2,1,0:T(8,128)(2,1)}), bf16[64,16,128]{2,1,0:T(8,128)(2,1)}, u32[]{:S(2)}, u32[]{:S(2)}) async-start(bf16[64,16,128]{2,1,0:T(8,128)(2,1)} %get-tuple-element.79), calls=%async_computation.4 | async-start | bytes 524288 | tf_op jit(solution)/shard_map/all_to_all | solution.py:782
  148.8 2.4 pad_maximum_fusion
  152.2 2.6 collective-permute-start.1
  156.4 20.6 %attend_back_first.1 = (bf16[16,304,128]{2,1,0:T(8,128)(2,1)}, bf16[1664,80]{1,0:T(8,128)(2,1)}, bf16[128,1664]{1,0:T(8,128)(2,1)}, f32[1664,128]{1,0:T(8,128)}) custom-call(bf16[16,624,128]{2,1,0:T(8,128)(2,1)} %copy-done.1, bf16[64,16,128]{2,1,0:T(8,128)(2,1)} %all-to-all-done.4.do_ref, bf16[1664,144]{1,0:T(8,128)(2,1)} %get-tuple-element.70.qa_ref, ...), custom_call_target="tpu_custom_call" | custom-call | flops 17999998976 | bytes 36000000 | tf_op jit(solution)/shard_map/attend_back_first/pallas_call | solution.py:308
  177.0 6.0 %all-to-all-start.5 = ((bf16[16,304,128]{2,1,0:T(8,128)(2,1)}), bf16[16,304,128]{2,1,0:T(8,128)(2,1)}, u32[]{:S(2)}, u32[]{:S(2)}) async-start(bf16[16,304,128]{2,1,0:T(8,128)(2,1)} %get-tuple-element.89), calls=%async_computation.5 | async-start | bytes 2490368 | tf_op jit(solution)/shard_map/all_to_all | solution.py:782
  183.0 19.6 %attend_back_second.1 = bf16[16,320,128]{2,1,0:T(8,128)(2,1)} custom-call(bf16[1664,144]{1,0:T(8,128)(2,1)} %get-tuple-element.70.qa_ref, bf16[1664,80]{1,0:T(8,128)(2,1)} %get-tuple-element.85.doa_ref, bf16[128,1664]{1,0:T(8,128)(2,1)} %get-tuple-element.86.turned_ref, f32[1664,128]{1,0:T(8,128)} %get-tuple-element.87.acc_in, ...), custom_call_target="tpu_custom_call" | custom-call | flops 17999998976 | bytes 36000000 | tf_op jit(solution)/shard_map/attend_back_second/pallas_call | solution.py:340
  202.6 3.7 %collective-permute-start.4 = (bf16[4080,128]{1,0:T(8,128)(2,1)}, bf16[4080,128]{1,0:T(8,128)(2,1)}, u32[]{:S(2)}, u32[]{:S(2)}) collective-permute-start(bf16[4080,128]{1,0:T(8,128)(2,1)} %get-tuple-element.98.refs_0_), channel_id=1, source_target_pairs={{0,64},{64,0},{1,65},{65,1},{2,66},{66,2},{3,67},{67,3},{4,68},{68... | collective-permute-start | bytes 3133448 | tf_op jit(solution)/shard_map/ppermute | solution.py:790
  206.9 6.9 %all-to-all-start.6 = ((bf16[16,320,128]{2,1,0:T(8,128)(2,1)}), bf16[16,320,128]{2,1,0:T(8,128)(2,1)}, u32[]{:S(2)}, u32[]{:S(2)}) async-start(bf16[16,320,128]{2,1,0:T(8,128)(2,1)} %attend_back_second.1), calls=%async_computation.6 | async-start | bytes 2621440 | tf_op jit(solution)/shard_map/all_to_all | solution.py:782
  213.9 6.9 %weight_grads.1 = bf16[16,384,128]{2,1,0:T(8,128)(2,1)} custom-call(s32[1]{0:T(128)} %bitcast.core_ref, bf16[4080,128]{1,0:T(8,128)(2,1)} %get-tuple-element.98.refs_0_, bf16[4080,128]{1,0:T(8,128)(2,1)} %collective-permute-done.refs_1_, bf16[4080,128]{1,0:T(8,128)(2,1)} %collective-permute-done.1.refs_2_, bf16[4080,128]{1,0:T(8,128)(2,1)} %collective-permute-done.2.refs_3_, ...), custom_call_target="tpu_custom_call" | custom-call | flops 1000000000 | bytes 2000000 | tf_op jit(solution)/shard_map/weight_grads/pallas_call | solution.py:608
  220.8 2.3 dynamic-slice_bitcast_fusion.6
  223.1 2.5 collective-permute-start.10
  227.4 6.5 %all-to-all-done.6.second_ref = bf16[16,320,128]{2,1,0:T(8,128)(2,1)} async-done(((bf16[16,320,128]{2,1,0:T(8,128)(2,1)}), bf16[16,320,128]{2,1,0:T(8,128)(2,1)}, u32[]{:S(2)}, u32[]{:S(2)}) %all-to-all-start.6) | async-done | bytes 1310752 | tf_op jit(solution)/shard_map/all_to_all | solution.py:782
  233.8 6.2 %project_back.1 = (bf16[4,768,128]{2,1,0:T(8,128)(2,1)}, bf16[16,128,128]{2,1,0:T(8,128)(2,1)}, bf16[16,128,128]{2,1,0:T(8,128)(2,1)}, bf16[48,2048]{1,0:T(8,128)(2,1)}) custom-call(s32[1]{0:T(128)} %bitcast.core_ref, bf16[16,304,128]{2,1,0:T(8,128)(2,1)} %all-to-all-done.5.first_ref, bf16[16,320,128]{2,1,0:T(8,128)(2,1)} %all-to-all-done.6.second_ref, ...), custom_call_target="tpu_custom_call" | custom-call | flops 5000000000 | bytes 10000000 | tf_op jit(solution)/shard_map/project_back/pallas_call | solution.py:678
  240.1 3.6 %all-to-all-start.7 = ((bf16[4,768,128]{2,1,0:T(8,128)(2,1)}), bf16[4,768,128]{2,1,0:T(8,128)(2,1)S(1)}, u32[]{:S(2)}, u32[]{:S(2)}) async-start(bf16[4,768,128]{2,1,0:T(8,128)(2,1)} %get-tuple-element.97), calls=%async_computation.7 | async-start | bytes 1572864 | tf_op jit(solution)/shard_map/all_to_all | solution.py:782
  243.7 2.4 collective-permute-start.3
  246.2 3.2 %collective-permute-done.9 = bf16[4,384,128]{2,1,0:T(8,128)(2,1)} collective-permute-done((bf16[4,384,128]{2,1,0:T(8,128)(2,1)}, bf16[4,384,128]{2,1,0:T(8,128)(2,1)}, u32[]{:S(2)}, u32[]{:S(2)}) %collective-permute-start.9) | collective-permute-done | bytes 393248 | tf_op jit(solution)/shard_map/ppermute | solution.py:786
  251.0 2.4 all-to-all-done.7.din_ref
  254.5 6.6 %all-to-all-start.8 = ((bf16[16,176,128]{2,1,0:T(8,128)(2,1)}), bf16[16,176,128]{2,1,0:T(8,128)(2,1)S(1)}, u32[]{:S(2)}, u32[]{:S(2)}) async-start(bf16[16,176,128]{2,1,0:T(8,128)(2,1)} %last_payload.1), calls=%async_computation.8 | async-start | bytes 1441792 | tf_op jit(solution)/shard_map/all_to_all | solution.py:782
  262.4 2.4 collective-permute-start.13
  266.0 8.2 %collective-permute-done.12 = bf16[384,128]{1,0:T(8,128)(2,1)S(1)} collective-permute-done((bf16[384,128]{1,0:T(8,128)(2,1)S(1)}, bf16[384,128]{1,0:T(8,128)(2,1)S(1)}, u32[]{:S(2)}, u32[]{:S(2)}) %collective-permute-start.12) | collective-permute-done | bytes 98336 | tf_op jit(solution)/shard_map/ppermute | solution.py:786
  275.0 2.9 %collective-permute-start.15 = (f32[384,128]{1,0:T(8,128)S(1)}, f32[384,128]{1,0:T(8,128)S(1)}, u32[]{:S(2)}, u32[]{:S(2)}) collective-permute-start(f32[384,128]{1,0:T(8,128)S(1)} %convert_add_fusion.1.wide_ref), channel_id=1, source_target_pairs={{0,64},{64,0},{1,65},{65,1},{2,66},{66,2},{3,67},{67,3},{4,68},{68... | collective-permute-start | bytes 589832 | tf_op jit(solution)/shard_map/ppermute | solution.py:790
  (95 shorter events, 28.8 us)
Async XLA Ops:
  7.2 18.5 %copy-start.10 = (f32[384]{0:T(512)S(1)}, f32[384]{0:T(512)}, u32[]{:S(2)}) copy-start(f32[384]{0:T(512)} %param.18) | copy-start | bytes 4612
  8.9 15.8 %all-to-all-start = ((bf16[16,48,128]{2,1,0:T(8,128)(2,1)}), bf16[16,48,128]{2,1,0:T(8,128)(2,1)S(1)}, u32[]{:S(2)}, u32[]{:S(2)}) async-start(bf16[16,48,128]{2,1,0:T(8,128)(2,1)} %bitcast_bitcast_fusion.1), calls=%async_computation | async-start | bytes 393216 | tf_op jit(solution)/shard_map/all_to_all | solution.py:782
  17.5 102.8 %all-gather.3.cloned.1.call-start = ((), (), s32[]{:S(2)}) async-start(), calls=%async_computation.9 | async-start | bytes 11096064 | tf_op jit(solution)/shard_map/all_gather | solution.py:850
  24.7 19.5 %copy-start.7 = (bf16[16,48,128]{2,1,0:T(8,128)(2,1)}, bf16[16,48,128]{2,1,0:T(8,128)(2,1)S(1)}, u32[]{:S(2)}) copy-start(bf16[16,48,128]{2,1,0:T(8,128)(2,1)S(1)} %all-to-all-done.x_ref) | copy-start | bytes 589828
  25.8 20.2 %all-to-all-start.1 = ((bf16[16,48,640]{2,1,0:T(8,128)(2,1)}), bf16[16,48,640]{2,1,0:T(8,128)(2,1)S(1)}, u32[]{:S(2)}, u32[]{:S(2)}) async-start(bf16[16,48,640]{2,1,0:T(8,128)(2,1)} %broadcast_in_dim.4), calls=%async_computation.1 | async-start | bytes 1966080 | tf_op jit(solution)/shard_map/all_to_all | solution.py:782
  48.6 39.3 %copy-start.4 = (s32[1,8192]{1,0:T(1,128)S(1)}, s32[1,8192]{1,0:T(1,128)}, u32[]{:S(2)}) copy-start(s32[1,8192]{1,0:T(1,128)} %param.16) | copy-start | bytes 98308
  48.6 39.3 %all-to-all-start.2 = ((bf16[16,624,128]{2,1,0:T(8,128)(2,1)}), bf16[16,624,128]{2,1,0:T(8,128)(2,1)S(1)}, u32[]{:S(2)}, u32[]{:S(2)}) async-start(bf16[16,624,128]{2,1,0:T(8,128)(2,1)} %project.1), calls=%async_computation.2 | async-start | bytes 5111808 | tf_op jit(solution)/shard_map/all_to_all | solution.py:782
  87.9 19.9 %copy-start.1 = (bf16[16,624,128]{2,1,0:T(8,128)(2,1)}, bf16[16,624,128]{2,1,0:T(8,128)(2,1)S(1)}, u32[]{:S(2)}) copy-start(bf16[16,624,128]{2,1,0:T(8,128)(2,1)S(1)} %all-to-all-done.2.q_ref.kv_ref.cot_ref) | copy-start | bytes 7667716
  107.8 21.5 %all-to-all-start.3 = ((bf16[64,16,128]{2,1,0:T(8,128)(2,1)}), bf16[64,16,128]{2,1,0:T(8,128)(2,1)}, u32[]{:S(2)}, u32[]{:S(2)}) async-start(bf16[64,16,128]{2,1,0:T(8,128)(2,1)} %get-tuple-element.71), calls=%async_computation.3 | async-start | bytes 524288 | tf_op jit(solution)/shard_map/all_to_all | solution.py:782
  141.6 14.8 %all-to-all-start.4 = ((bf16[64,16,128]{2,1,0:T(8,128)(2,1)}), bf16[64,16,128]{2,1,0:T(8,128)(2,1)}, u32[]{:S(2)}, u32[]{:S(2)}) async-start(bf16[64,16,128]{2,1,0:T(8,128)(2,1)} %get-tuple-element.79), calls=%async_computation.4 | async-start | bytes 524288 | tf_op jit(solution)/shard_map/all_to_all | solution.py:782
  151.2 51.4 %collective-permute-start = (bf16[4080,128]{1,0:T(8,128)(2,1)}, bf16[4080,128]{1,0:T(8,128)(2,1)}, u32[]{:S(2)}, u32[]{:S(2)}) collective-permute-start(bf16[4080,128]{1,0:T(8,128)(2,1)} %get-tuple-element.128), channel_id=1, source_target_pairs={{0,16},{16,32},{32,48},{48,0},{1,17},{17,33},{33,49},{49,1},{2,18}... | collective-permute-start | bytes 3133448 | tf_op jit(solution)/shard_map/ppermute | solution.py:786
  152.2 50.4 %collective-permute-start.1 = (bf16[4080,128]{1,0:T(8,128)(2,1)}, bf16[4080,128]{1,0:T(8,128)(2,1)}, u32[]{:S(2)}, u32[]{:S(2)}) collective-permute-start(bf16[4080,128]{1,0:T(8,128)(2,1)} %get-tuple-element.129), channel_id=1, source_target_pairs={{0,32},{16,48},{32,0},{48,16},{1,33},{17,49},{33,1},{49,17},{2,34}... | collective-permute-start | bytes 3133448 | tf_op jit(solution)/shard_map/ppermute | solution.py:786
  154.8 47.8 %collective-permute-start.2 = (bf16[4080,128]{1,0:T(8,128)(2,1)}, bf16[4080,128]{1,0:T(8,128)(2,1)}, u32[]{:S(2)}, u32[]{:S(2)}) collective-permute-start(bf16[4080,128]{1,0:T(8,128)(2,1)} %get-tuple-element.127), channel_id=1, source_target_pairs={{0,48},{16,0},{32,16},{48,32},{1,49},{17,1},{33,17},{49,33},{2,50}... | collective-permute-start | bytes 3133448 | tf_op jit(solution)/shard_map/ppermute | solution.py:786
  177.0 25.6 %all-to-all-start.5 = ((bf16[16,304,128]{2,1,0:T(8,128)(2,1)}), bf16[16,304,128]{2,1,0:T(8,128)(2,1)}, u32[]{:S(2)}, u32[]{:S(2)}) async-start(bf16[16,304,128]{2,1,0:T(8,128)(2,1)} %get-tuple-element.89), calls=%async_computation.5 | async-start | bytes 2490368 | tf_op jit(solution)/shard_map/all_to_all | solution.py:782
  202.6 11.2 %collective-permute-start.4 = (bf16[4080,128]{1,0:T(8,128)(2,1)}, bf16[4080,128]{1,0:T(8,128)(2,1)}, u32[]{:S(2)}, u32[]{:S(2)}) collective-permute-start(bf16[4080,128]{1,0:T(8,128)(2,1)} %get-tuple-element.98.refs_0_), channel_id=1, source_target_pairs={{0,64},{64,0},{1,65},{65,1},{2,66},{66,2},{3,67},{67,3},{4,68},{68... | collective-permute-start | bytes 3133448 | tf_op jit(solution)/shard_map/ppermute | solution.py:790
  206.3 7.6 %collective-permute-start.5 = (bf16[4080,128]{1,0:T(8,128)(2,1)}, bf16[4080,128]{1,0:T(8,128)(2,1)}, u32[]{:S(2)}, u32[]{:S(2)}) collective-permute-start(bf16[4080,128]{1,0:T(8,128)(2,1)} %collective-permute-done.refs_1_), channel_id=1, source_target_pairs={{0,64},{64,0},{1,65},{65,1},{2,66},{66,2},{3,67},{67,3},{4,68},{68... | collective-permute-start | bytes 3133448 | tf_op jit(solution)/shard_map/ppermute | solution.py:790
  206.4 7.5 %collective-permute-start.6 = (bf16[4080,128]{1,0:T(8,128)(2,1)}, bf16[4080,128]{1,0:T(8,128)(2,1)}, u32[]{:S(2)}, u32[]{:S(2)}) collective-permute-start(bf16[4080,128]{1,0:T(8,128)(2,1)} %collective-permute-done.1.refs_2_), channel_id=1, source_target_pairs={{0,64},{64,0},{1,65},{65,1},{2,66},{66,2},{3,67},{67,3},{4,68},{68... | collective-permute-start | bytes 3133448 | tf_op jit(solution)/shard_map/ppermute | solution.py:790
  206.8 7.1 %collective-permute-start.7 = (bf16[4080,128]{1,0:T(8,128)(2,1)}, bf16[4080,128]{1,0:T(8,128)(2,1)}, u32[]{:S(2)}, u32[]{:S(2)}) collective-permute-start(bf16[4080,128]{1,0:T(8,128)(2,1)} %collective-permute-done.2.refs_3_), channel_id=1, source_target_pairs={{0,64},{64,0},{1,65},{65,1},{2,66},{66,2},{3,67},{67,3},{4,68},{68... | collective-permute-start | bytes 3133448 | tf_op jit(solution)/shard_map/ppermute | solution.py:790
  206.9 26.9 %all-to-all-start.6 = ((bf16[16,320,128]{2,1,0:T(8,128)(2,1)}), bf16[16,320,128]{2,1,0:T(8,128)(2,1)}, u32[]{:S(2)}, u32[]{:S(2)}) async-start(bf16[16,320,128]{2,1,0:T(8,128)(2,1)} %attend_back_second.1), calls=%async_computation.6 | async-start | bytes 2621440 | tf_op jit(solution)/shard_map/all_to_all | solution.py:782
  223.1 23.0 %collective-permute-start.10 = (bf16[4,384,128]{2,1,0:T(8,128)(2,1)}, bf16[4,384,128]{2,1,0:T(8,128)(2,1)}, u32[]{:S(2)}, u32[]{:S(2)}) collective-permute-start(bf16[4,384,128]{2,1,0:T(8,128)(2,1)} %get-tuple-element.125), channel_id=1, source_target_pairs={{0,12},{4,0},{8,4},{12,8},{1,13},{5,1},{9,5},{13,9},{2,14},{6,2},{... | collective-permute-start | bytes 1179656 | tf_op jit(solution)/shard_map/ppermute | solution.py:786
  225.6 20.5 %collective-permute-start.8 = (bf16[4,384,128]{2,1,0:T(8,128)(2,1)}, bf16[4,384,128]{2,1,0:T(8,128)(2,1)}, u32[]{:S(2)}, u32[]{:S(2)}) collective-permute-start(bf16[4,384,128]{2,1,0:T(8,128)(2,1)} %get-tuple-element.124), channel_id=1, source_target_pairs={{0,4},{4,8},{8,12},{12,0},{1,5},{5,9},{9,13},{13,1},{2,6},{6,10},{... | collective-permute-start | bytes 1179656 | tf_op jit(solution)/shard_map/ppermute | solution.py:786
  225.6 23.7 %collective-permute-start.9 = (bf16[4,384,128]{2,1,0:T(8,128)(2,1)}, bf16[4,384,128]{2,1,0:T(8,128)(2,1)}, u32[]{:S(2)}, u32[]{:S(2)}) collective-permute-start(bf16[4,384,128]{2,1,0:T(8,128)(2,1)} %get-tuple-element.126), channel_id=1, source_target_pairs={{0,8},{4,12},{8,0},{12,4},{1,9},{5,13},{9,1},{13,5},{2,10},{6,14},... | collective-permute-start | bytes 1179656 | tf_op jit(solution)/shard_map/ppermute | solution.py:786
  240.1 13.3 %copy-start.5 = (bf16[16,128,128]{2,1,0:T(8,128)(2,1)S(1)}, bf16[16,128,128]{2,1,0:T(8,128)(2,1)}, u32[]{:S(2)}) copy-start(bf16[16,128,128]{2,1,0:T(8,128)(2,1)} %get-tuple-element.95.mine_ref) | copy-start | bytes 1572868
  240.1 13.3 %copy-start.6 = (f32[768,128]{1,0:T(8,128)S(1)}, f32[768,128]{1,0:T(8,128)}, u32[]{:S(2)}) copy-start(f32[768,128]{1,0:T(8,128)} %get-tuple-element.103.dh1_ref) | copy-start | bytes 1179652
  240.1 13.3 %all-to-all-start.7 = ((bf16[4,768,128]{2,1,0:T(8,128)(2,1)}), bf16[4,768,128]{2,1,0:T(8,128)(2,1)S(1)}, u32[]{:S(2)}, u32[]{:S(2)}) async-start(bf16[4,768,128]{2,1,0:T(8,128)(2,1)} %get-tuple-element.97), calls=%async_computation.7 | async-start | bytes 1572864 | tf_op jit(solution)/shard_map/all_to_all | solution.py:782
  243.7 9.6 %collective-permute-start.3 = (bf16[16,128,128]{2,1,0:T(8,128)(2,1)}, bf16[16,128,128]{2,1,0:T(8,128)(2,1)S(1)}, u32[]{:S(2)}, u32[]{:S(2)}) collective-permute-start(bf16[16,128,128]{2,1,0:T(8,128)(2,1)} %get-tuple-element.96), channel_id=1, source_target_pairs={{0,64},{64,0},{1,65},{65,1},{2,66},{66,2},{3,67},{67,3},{4,68},{68... | collective-permute-start | bytes 1572872 | tf_op jit(solution)/shard_map/ppermute | solution.py:790
  254.5 25.4 %all-to-all-start.8 = ((bf16[16,176,128]{2,1,0:T(8,128)(2,1)}), bf16[16,176,128]{2,1,0:T(8,128)(2,1)S(1)}, u32[]{:S(2)}, u32[]{:S(2)}) async-start(bf16[16,176,128]{2,1,0:T(8,128)(2,1)} %last_payload.1), calls=%async_computation.8 | async-start | bytes 1441792 | tf_op jit(solution)/shard_map/all_to_all | solution.py:782
  261.1 13.1 %collective-permute-start.12 = (bf16[384,128]{1,0:T(8,128)(2,1)S(1)}, bf16[384,128]{1,0:T(8,128)(2,1)S(1)}, u32[]{:S(2)}, u32[]{:S(2)}) collective-permute-start(bf16[384,128]{1,0:T(8,128)(2,1)S(1)} %get-tuple-element.107), channel_id=1, source_target_pairs={{0,1},{1,2},{2,3},{3,0},{4,5},{5,6},{6,7},{7,4},{8,9},{9,10},{10,1... | collective-permute-start | bytes 294920 | tf_op jit(solution)/shard_map/ppermute | solution.py:786
  262.4 12.5 %collective-permute-start.13 = (bf16[384,128]{1,0:T(8,128)(2,1)S(1)}, bf16[384,128]{1,0:T(8,128)(2,1)S(1)}, u32[]{:S(2)}, u32[]{:S(2)}) collective-permute-start(bf16[384,128]{1,0:T(8,128)(2,1)S(1)} %get-tuple-element.108), channel_id=1, source_target_pairs={{0,2},{1,3},{2,0},{3,1},{4,6},{5,7},{6,4},{7,5},{8,10},{9,11},{10,... | collective-permute-start | bytes 294920 | tf_op jit(solution)/shard_map/ppermute | solution.py:786
  264.8 10.1 %collective-permute-start.14 = (bf16[384,128]{1,0:T(8,128)(2,1)S(1)}, bf16[384,128]{1,0:T(8,128)(2,1)S(1)}, u32[]{:S(2)}, u32[]{:S(2)}) collective-permute-start(bf16[384,128]{1,0:T(8,128)(2,1)S(1)} %get-tuple-element.109), channel_id=1, source_target_pairs={{0,3},{1,0},{2,1},{3,2},{4,7},{5,4},{6,5},{7,6},{8,11},{9,8},{10,9... | collective-permute-start | bytes 294920 | tf_op jit(solution)/shard_map/ppermute | solution.py:786
  275.0 4.0 %collective-permute-start.15 = (f32[384,128]{1,0:T(8,128)S(1)}, f32[384,128]{1,0:T(8,128)S(1)}, u32[]{:S(2)}, u32[]{:S(2)}) collective-permute-start(f32[384,128]{1,0:T(8,128)S(1)} %convert_add_fusion.1.wide_ref), channel_id=1, source_target_pairs={{0,64},{64,0},{1,65},{65,1},{2,66},{66,2},{3,67},{67,3},{4,68},{68... | collective-permute-start | bytes 589832 | tf_op jit(solution)/shard_map/ppermute | solution.py:790
  279.9 1.4 collective-permute-start.11
  (5 other events, 38.6 us)
Sparse Core Ops, SparseCore 0:
  25.9 94.0 all-gather.2

commit v2 on v1

--- a/solution.py
+++ b/solution.py
@@ -27,7 +27,7 @@
 JW = 640
 HALF = 2
 FWD_C = 2
-BWD_C = 2
+BWD_C = 1
 Q_AT = NROW * TOK
 C_AT = Q_AT + 64
 BLOCK = C_AT + 48

time: 290 us -> 293 us (1.010)
  Pallas kernels: 90.9 us -> 94.2 us
where the time goes in v2:
time: 293 us; the launch traced here: 292 us
  Pallas kernels  94.2 us (32%)
  starting transfers between devices  84.3 us (29%)
  waiting for transfers between devices  67.1 us (23%)
  between operations  14.4 us (5%)
  blocking collectives  12.7 us (4%)
  local copies, waits for them, and re-layouts  11.6 us (4%)
  other arithmetic  7.76 us (3%)
    all_to_all x9, starting transfers between devices, exchange(): return lax.all_to_all(blocks, axis, 0, 0, tiled=True)  60.2 us
    all_to_all x9, waiting for transfers between devices, exchange(): return lax.all_to_all(blocks, axis, 0, 0, tiled=True)  54 us
    pallas_call x1, Pallas kernels, attend_back_first(): pl.pallas_call(back_first_kernel, grid=(BACK_STEPS,), out_shape=(pltpu.HB...  22.4 us
    pallas_call x1, Pallas kernels, attend_back_second(): pl.pallas_call(back_second_kernel, grid=(BACK_STEPS,), out_shape=pltpu.HB...  21.1 us
    pallas_call x1, Pallas kernels, attend(): pl.pallas_call(attend_kernel, grid=(NCOL // FWD_C,), out_shape=(pltpu.HBM...  19.9 us
    ppermute x9, starting transfers between devices, around(): return lax.ppermute(v, axis, [(i, (i + shift) % 4) for i in range(4)])  13.8 us
    all_gather x1, blocking collectives, per_device(): x4 = lax.all_gather(x_t.reshape(DIM, TOK), 'row', axis=0, tiled=False)  12.7 us
    pallas_call x1, Pallas kernels, tokenwise(): pl.pallas_call(tokenwise_kernel, out_shape=(pltpu.HBM((SAME, TOK), BF), p...  12.3 us
  transfers between devices with their start and end apart: 26, of which 12 were waited for; matrix products, arithmetic and copies ran while one was open for 6% of the time, Pallas kernels for 27%

profile of v2, /device:TPU:1, one launch (start us, length us, event | category | flops | bytes accessed | tf_op | source)
XLA Modules:
  0.0 292.2 jit_solution(7816133152695696656)
XLA Ops:
  8.9 8.6 %all-to-all-start = ((bf16[16,48,128]{2,1,0:T(8,128)(2,1)}), bf16[16,48,128]{2,1,0:T(8,128)(2,1)S(1)}, u32[]{:S(2)}, u32[]{:S(2)}) async-start(bf16[16,48,128]{2,1,0:T(8,128)(2,1)} %bitcast_bitcast_fusion.1), calls=%async_computation | async-start | bytes 393216 | tf_op jit(solution)/shard_map/all_to_all | solution.py:782
  25.8 5.2 %all-to-all-start.1 = ((bf16[16,48,640]{2,1,0:T(8,128)(2,1)}), bf16[16,48,640]{2,1,0:T(8,128)(2,1)S(1)}, u32[]{:S(2)}, u32[]{:S(2)}) async-start(bf16[16,48,640]{2,1,0:T(8,128)(2,1)} %broadcast_in_dim.4), calls=%async_computation.1 | async-start | bytes 1966080 | tf_op jit(solution)/shard_map/all_to_all | solution.py:782
  31.4 12.7 %all_gather.9.x_ref = bf16[4,768,128]{2,1,0:T(8,128)(2,1)S(1)} all-gather(bf16[1,768,128]{2,1,0:T(8,128)(2,1)S(1)} %bitcast.95), channel_id=1, replica_groups=mesh['dp'=2,'row'=4,'z'=4,'y'=4] {'row'}, dimensions={0}, use_global_device_ids=true | all-gather | bytes 983040 | tf_op jit(solution)/shard_map/all_gather | solution.py:834
  44.1 2.0 all-to-all-done.1.w_ref.vec_ref
  46.1 2.5 project.1
  48.6 5.2 %all-to-all-start.2 = ((bf16[16,624,128]{2,1,0:T(8,128)(2,1)}), bf16[16,624,128]{2,1,0:T(8,128)(2,1)S(1)}, u32[]{:S(2)}, u32[]{:S(2)}) async-start(bf16[16,624,128]{2,1,0:T(8,128)(2,1)} %project.1), calls=%async_computation.2 | async-start | bytes 5111808 | tf_op jit(solution)/shard_map/all_to_all | solution.py:782
  53.8 34.1 %all-to-all-done.2.q_ref.kv_ref.cot_ref = bf16[16,624,128]{2,1,0:T(8,128)(2,1)S(1)} async-done(((bf16[16,624,128]{2,1,0:T(8,128)(2,1)}), bf16[16,624,128]{2,1,0:T(8,128)(2,1)S(1)}, u32[]{:S(2)}, u32[]{:S(2)}) %all-to-all-start.2) | async-done | bytes 2555936 | tf_op jit(solution)/shard_map/all_to_all | solution.py:782
  87.9 19.9 %attend.1 = (bf16[1664,144]{1,0:T(8,128)(2,1)}, f32[1664,64]{1,0:T(8,128)}, bf16[64,16,128]{2,1,0:T(8,128)(2,1)}) custom-call(s32[1]{0:T(128)} %bitcast.1.shift_ref, bf16[16,624,128]{2,1,0:T(8,128)(2,1)S(1)} %all-to-all-done.2.q_ref.kv_ref.cot_ref, bf16[16,624,128]{2,1,0:T(8,128)(2,1)S(1)} %all-to-all-done.2.q_ref.kv_ref.cot_ref, s32[64,128]{1,0:T(8,128)S(1)} %bitcast.92), custom_call_target="tpu_custom_call" | custom-call | flops 20000000000 | bytes 40000000 | tf_op jit(solution)/shard_map/attend/pallas_call | solution.py:212
  107.8 12.5 %all-to-all-start.3 = ((bf16[64,16,128]{2,1,0:T(8,128)(2,1)}), bf16[64,16,128]{2,1,0:T(8,128)(2,1)}, u32[]{:S(2)}, u32[]{:S(2)}) async-start(bf16[64,16,128]{2,1,0:T(8,128)(2,1)} %get-tuple-element.71), calls=%async_computation.3 | async-start | bytes 524288 | tf_op jit(solution)/shard_map/all_to_all | solution.py:782
  122.2 7.0 %all-to-all-done.3.att_ref = bf16[64,16,128]{2,1,0:T(8,128)(2,1)} async-done(((bf16[64,16,128]{2,1,0:T(8,128)(2,1)}), bf16[64,16,128]{2,1,0:T(8,128)(2,1)}, u32[]{:S(2)}, u32[]{:S(2)}) %all-to-all-start.3) | async-done | bytes 262176 | tf_op jit(solution)/shard_map/all_to_all | solution.py:782
  129.3 12.3 %tokenwise.1 = (bf16[2352,128]{1,0:T(8,128)(2,1)}, bf16[4,1728,128]{2,1,0:T(8,128)(2,1)}, bf16[64,16,128]{2,1,0:T(8,128)(2,1)}, bf16[16,48,128]{2,1,0:T(8,128)(2,1)}, f32[768,128]{1,0:T(8,128)}) custom-call(s32[1]{0:T(128)} %bitcast.13.row_ref, bf16[64,16,128]{2,1,0:T(8,128)(2,1)} %all-to-all-done.3.att_ref, bf16[16,48,128]{2,1,0:T(8,128)(2,1)} %copy-done.7, ...), custom_call_target="tpu_custom_call" | custom-call | flops 15000000512 | bytes 30000000 | tf_op jit(solution)/shard_map/tokenwise/pallas_call | solution.py:512
  141.6 5.6 %all-to-all-start.4 = ((bf16[64,16,128]{2,1,0:T(8,128)(2,1)}), bf16[64,16,128]{2,1,0:T(8,128)(2,1)}, u32[]{:S(2)}, u32[]{:S(2)}) async-start(bf16[64,16,128]{2,1,0:T(8,128)(2,1)} %get-tuple-element.79), calls=%async_computation.4 | async-start | bytes 524288 | tf_op jit(solution)/shard_map/all_to_all | solution.py:782
  148.8 2.4 pad_maximum_fusion
  152.2 2.6 collective-permute-start.1
  156.4 22.4 %attend_back_first.1 = (bf16[16,304,128]{2,1,0:T(8,128)(2,1)}, bf16[1664,80]{1,0:T(8,128)(2,1)}, bf16[128,1664]{1,0:T(8,128)(2,1)}, f32[1664,128]{1,0:T(8,128)}) custom-call(bf16[16,624,128]{2,1,0:T(8,128)(2,1)} %copy-done.1, bf16[64,16,128]{2,1,0:T(8,128)(2,1)} %all-to-all-done.4.do_ref, bf16[1664,144]{1,0:T(8,128)(2,1)} %get-tuple-element.70.qa_ref, ...), custom_call_target="tpu_custom_call" | custom-call | flops 17999998976 | bytes 36000000 | tf_op jit(solution)/shard_map/attend_back_first/pallas_call | solution.py:308
  178.8 6.0 %all-to-all-start.5 = ((bf16[16,304,128]{2,1,0:T(8,128)(2,1)}), bf16[16,304,128]{2,1,0:T(8,128)(2,1)}, u32[]{:S(2)}, u32[]{:S(2)}) async-start(bf16[16,304,128]{2,1,0:T(8,128)(2,1)} %get-tuple-element.89), calls=%async_computation.5 | async-start | bytes 2490368 | tf_op jit(solution)/shard_map/all_to_all | solution.py:782
  184.8 21.1 %attend_back_second.1 = bf16[16,320,128]{2,1,0:T(8,128)(2,1)} custom-call(bf16[1664,144]{1,0:T(8,128)(2,1)} %get-tuple-element.70.qa_ref, bf16[1664,80]{1,0:T(8,128)(2,1)} %get-tuple-element.85.doa_ref, bf16[128,1664]{1,0:T(8,128)(2,1)} %get-tuple-element.86.turned_ref, f32[1664,128]{1,0:T(8,128)} %get-tuple-element.87.acc_in, ...), custom_call_target="tpu_custom_call" | custom-call | flops 17999998976 | bytes 36000000 | tf_op jit(solution)/shard_map/attend_back_second/pallas_call | solution.py:340
  205.9 3.7 %collective-permute-start.4 = (bf16[4080,128]{1,0:T(8,128)(2,1)}, bf16[4080,128]{1,0:T(8,128)(2,1)}, u32[]{:S(2)}, u32[]{:S(2)}) collective-permute-start(bf16[4080,128]{1,0:T(8,128)(2,1)} %get-tuple-element.98.refs_0_), channel_id=1, source_target_pairs={{0,64},{64,0},{1,65},{65,1},{2,66},{66,2},{3,67},{67,3},{4,68},{68... | collective-permute-start | bytes 3133448 | tf_op jit(solution)/shard_map/ppermute | solution.py:790
  210.2 6.9 %all-to-all-start.6 = ((bf16[16,320,128]{2,1,0:T(8,128)(2,1)}), bf16[16,320,128]{2,1,0:T(8,128)(2,1)}, u32[]{:S(2)}, u32[]{:S(2)}) async-start(bf16[16,320,128]{2,1,0:T(8,128)(2,1)} %attend_back_second.1), calls=%async_computation.6 | async-start | bytes 2621440 | tf_op jit(solution)/shard_map/all_to_all | solution.py:782
  217.2 6.9 %weight_grads.1 = bf16[16,384,128]{2,1,0:T(8,128)(2,1)} custom-call(s32[1]{0:T(128)} %bitcast.core_ref, bf16[4080,128]{1,0:T(8,128)(2,1)} %get-tuple-element.98.refs_0_, bf16[4080,128]{1,0:T(8,128)(2,1)} %collective-permute-done.refs_1_, bf16[4080,128]{1,0:T(8,128)(2,1)} %collective-permute-done.1.refs_2_, bf16[4080,128]{1,0:T(8,128)(2,1)} %collective-permute-done.2.refs_3_, ...), custom_call_target="tpu_custom_call" | custom-call | flops 1000000000 | bytes 2000000 | tf_op jit(solution)/shard_map/weight_grads/pallas_call | solution.py:608
  224.1 2.3 dynamic-slice_bitcast_fusion.6
  226.4 2.5 collective-permute-start.10
  230.7 6.5 %all-to-all-done.6.second_ref = bf16[16,320,128]{2,1,0:T(8,128)(2,1)} async-done(((bf16[16,320,128]{2,1,0:T(8,128)(2,1)}), bf16[16,320,128]{2,1,0:T(8,128)(2,1)}, u32[]{:S(2)}, u32[]{:S(2)}) %all-to-all-start.6) | async-done | bytes 1310752 | tf_op jit(solution)/shard_map/all_to_all | solution.py:782
  237.1 6.2 %project_back.1 = (bf16[4,768,128]{2,1,0:T(8,128)(2,1)}, bf16[16,128,128]{2,1,0:T(8,128)(2,1)}, bf16[16,128,128]{2,1,0:T(8,128)(2,1)}, bf16[48,2048]{1,0:T(8,128)(2,1)}) custom-call(s32[1]{0:T(128)} %bitcast.core_ref, bf16[16,304,128]{2,1,0:T(8,128)(2,1)} %all-to-all-done.5.first_ref, bf16[16,320,128]{2,1,0:T(8,128)(2,1)} %all-to-all-done.6.second_ref, ...), custom_call_target="tpu_custom_call" | custom-call | flops 5000000000 | bytes 10000000 | tf_op jit(solution)/shard_map/project_back/pallas_call | solution.py:678
  243.4 3.6 %all-to-all-start.7 = ((bf16[4,768,128]{2,1,0:T(8,128)(2,1)}), bf16[4,768,128]{2,1,0:T(8,128)(2,1)S(1)}, u32[]{:S(2)}, u32[]{:S(2)}) async-start(bf16[4,768,128]{2,1,0:T(8,128)(2,1)} %get-tuple-element.97), calls=%async_computation.7 | async-start | bytes 1572864 | tf_op jit(solution)/shard_map/all_to_all | solution.py:782
  247.0 2.7 collective-permute-start.3
  249.7 3.0 %collective-permute-done.9 = bf16[4,384,128]{2,1,0:T(8,128)(2,1)} collective-permute-done((bf16[4,384,128]{2,1,0:T(8,128)(2,1)}, bf16[4,384,128]{2,1,0:T(8,128)(2,1)}, u32[]{:S(2)}, u32[]{:S(2)}) %collective-permute-start.9) | collective-permute-done | bytes 393248 | tf_op jit(solution)/shard_map/ppermute | solution.py:786
  254.3 2.4 all-to-all-done.7.din_ref
  257.8 6.6 %all-to-all-start.8 = ((bf16[16,176,128]{2,1,0:T(8,128)(2,1)}), bf16[16,176,128]{2,1,0:T(8,128)(2,1)S(1)}, u32[]{:S(2)}, u32[]{:S(2)}) async-start(bf16[16,176,128]{2,1,0:T(8,128)(2,1)} %last_payload.1), calls=%async_computation.8 | async-start | bytes 1441792 | tf_op jit(solution)/shard_map/all_to_all | solution.py:782
  265.7 2.4 collective-permute-start.13
  269.3 8.2 %collective-permute-done.12 = bf16[384,128]{1,0:T(8,128)(2,1)S(1)} collective-permute-done((bf16[384,128]{1,0:T(8,128)(2,1)S(1)}, bf16[384,128]{1,0:T(8,128)(2,1)S(1)}, u32[]{:S(2)}, u32[]{:S(2)}) %collective-permute-start.12) | collective-permute-done | bytes 98336 | tf_op jit(solution)/shard_map/ppermute | solution.py:786
  278.3 2.9 collective-permute-start.15
  (95 shorter events, 28.8 us)
Async XLA Ops:
  7.2 18.5 %copy-start.10 = (f32[384]{0:T(512)S(1)}, f32[384]{0:T(512)}, u32[]{:S(2)}) copy-start(f32[384]{0:T(512)} %param.18) | copy-start | bytes 4612
  8.9 15.8 %all-to-all-start = ((bf16[16,48,128]{2,1,0:T(8,128)(2,1)}), bf16[16,48,128]{2,1,0:T(8,128)(2,1)S(1)}, u32[]{:S(2)}, u32[]{:S(2)}) async-start(bf16[16,48,128]{2,1,0:T(8,128)(2,1)} %bitcast_bitcast_fusion.1), calls=%async_computation | async-start | bytes 393216 | tf_op jit(solution)/shard_map/all_to_all | solution.py:782
  17.5 102.8 %all-gather.3.cloned.1.call-start = ((), (), s32[]{:S(2)}) async-start(), calls=%async_computation.9 | async-start | bytes 11096064 | tf_op jit(solution)/shard_map/all_gather | solution.py:850
  24.7 19.5 %copy-start.7 = (bf16[16,48,128]{2,1,0:T(8,128)(2,1)}, bf16[16,48,128]{2,1,0:T(8,128)(2,1)S(1)}, u32[]{:S(2)}) copy-start(bf16[16,48,128]{2,1,0:T(8,128)(2,1)S(1)} %all-to-all-done.x_ref) | copy-start | bytes 589828
  25.8 20.2 %all-to-all-start.1 = ((bf16[16,48,640]{2,1,0:T(8,128)(2,1)}), bf16[16,48,640]{2,1,0:T(8,128)(2,1)S(1)}, u32[]{:S(2)}, u32[]{:S(2)}) async-start(bf16[16,48,640]{2,1,0:T(8,128)(2,1)} %broadcast_in_dim.4), calls=%async_computation.1 | async-start | bytes 1966080 | tf_op jit(solution)/shard_map/all_to_all | solution.py:782
  48.6 39.3 %copy-start.4 = (s32[1,8192]{1,0:T(1,128)S(1)}, s32[1,8192]{1,0:T(1,128)}, u32[]{:S(2)}) copy-start(s32[1,8192]{1,0:T(1,128)} %param.16) | copy-start | bytes 98308
  48.6 39.3 %all-to-all-start.2 = ((bf16[16,624,128]{2,1,0:T(8,128)(2,1)}), bf16[16,624,128]{2,1,0:T(8,128)(2,1)S(1)}, u32[]{:S(2)}, u32[]{:S(2)}) async-start(bf16[16,624,128]{2,1,0:T(8,128)(2,1)} %project.1), calls=%async_computation.2 | async-start | bytes 5111808 | tf_op jit(solution)/shard_map/all_to_all | solution.py:782
  87.9 19.9 %copy-start.1 = (bf16[16,624,128]{2,1,0:T(8,128)(2,1)}, bf16[16,624,128]{2,1,0:T(8,128)(2,1)S(1)}, u32[]{:S(2)}) copy-start(bf16[16,624,128]{2,1,0:T(8,128)(2,1)S(1)} %all-to-all-done.2.q_ref.kv_ref.cot_ref) | copy-start | bytes 7667716
  107.8 21.5 %all-to-all-start.3 = ((bf16[64,16,128]{2,1,0:T(8,128)(2,1)}), bf16[64,16,128]{2,1,0:T(8,128)(2,1)}, u32[]{:S(2)}, u32[]{:S(2)}) async-start(bf16[64,16,128]{2,1,0:T(8,128)(2,1)} %get-tuple-element.71), calls=%async_computation.3 | async-start | bytes 524288 | tf_op jit(solution)/shard_map/all_to_all | solution.py:782
  141.6 14.8 %all-to-all-start.4 = ((bf16[64,16,128]{2,1,0:T(8,128)(2,1)}), bf16[64,16,128]{2,1,0:T(8,128)(2,1)}, u32[]{:S(2)}, u32[]{:S(2)}) async-start(bf16[64,16,128]{2,1,0:T(8,128)(2,1)} %get-tuple-element.79), calls=%async_computation.4 | async-start | bytes 524288 | tf_op jit(solution)/shard_map/all_to_all | solution.py:782
  151.2 54.6 %collective-permute-start = (bf16[4080,128]{1,0:T(8,128)(2,1)}, bf16[4080,128]{1,0:T(8,128)(2,1)}, u32[]{:S(2)}, u32[]{:S(2)}) collective-permute-start(bf16[4080,128]{1,0:T(8,128)(2,1)} %get-tuple-element.128), channel_id=1, source_target_pairs={{0,16},{16,32},{32,48},{48,0},{1,17},{17,33},{33,49},{49,1},{2,18}... | collective-permute-start | bytes 3133448 | tf_op jit(solution)/shard_map/ppermute | solution.py:786
  152.2 53.7 %collective-permute-start.1 = (bf16[4080,128]{1,0:T(8,128)(2,1)}, bf16[4080,128]{1,0:T(8,128)(2,1)}, u32[]{:S(2)}, u32[]{:S(2)}) collective-permute-start(bf16[4080,128]{1,0:T(8,128)(2,1)} %get-tuple-element.129), channel_id=1, source_target_pairs={{0,32},{16,48},{32,0},{48,16},{1,33},{17,49},{33,1},{49,17},{2,34}... | collective-permute-start | bytes 3133448 | tf_op jit(solution)/shard_map/ppermute | solution.py:786
  154.8 51.1 %collective-permute-start.2 = (bf16[4080,128]{1,0:T(8,128)(2,1)}, bf16[4080,128]{1,0:T(8,128)(2,1)}, u32[]{:S(2)}, u32[]{:S(2)}) collective-permute-start(bf16[4080,128]{1,0:T(8,128)(2,1)} %get-tuple-element.127), channel_id=1, source_target_pairs={{0,48},{16,0},{32,16},{48,32},{1,49},{17,1},{33,17},{49,33},{2,50}... | collective-permute-start | bytes 3133448 | tf_op jit(solution)/shard_map/ppermute | solution.py:786
  178.8 27.1 %all-to-all-start.5 = ((bf16[16,304,128]{2,1,0:T(8,128)(2,1)}), bf16[16,304,128]{2,1,0:T(8,128)(2,1)}, u32[]{:S(2)}, u32[]{:S(2)}) async-start(bf16[16,304,128]{2,1,0:T(8,128)(2,1)} %get-tuple-element.89), calls=%async_computation.5 | async-start | bytes 2490368 | tf_op jit(solution)/shard_map/all_to_all | solution.py:782
  205.9 11.2 %collective-permute-start.4 = (bf16[4080,128]{1,0:T(8,128)(2,1)}, bf16[4080,128]{1,0:T(8,128)(2,1)}, u32[]{:S(2)}, u32[]{:S(2)}) collective-permute-start(bf16[4080,128]{1,0:T(8,128)(2,1)} %get-tuple-element.98.refs_0_), channel_id=1, source_target_pairs={{0,64},{64,0},{1,65},{65,1},{2,66},{66,2},{3,67},{67,3},{4,68},{68... | collective-permute-start | bytes 3133448 | tf_op jit(solution)/shard_map/ppermute | solution.py:790
  209.6 7.6 %collective-permute-start.5 = (bf16[4080,128]{1,0:T(8,128)(2,1)}, bf16[4080,128]{1,0:T(8,128)(2,1)}, u32[]{:S(2)}, u32[]{:S(2)}) collective-permute-start(bf16[4080,128]{1,0:T(8,128)(2,1)} %collective-permute-done.refs_1_), channel_id=1, source_target_pairs={{0,64},{64,0},{1,65},{65,1},{2,66},{66,2},{3,67},{67,3},{4,68},{68... | collective-permute-start | bytes 3133448 | tf_op jit(solution)/shard_map/ppermute | solution.py:790
  209.7 7.5 %collective-permute-start.6 = (bf16[4080,128]{1,0:T(8,128)(2,1)}, bf16[4080,128]{1,0:T(8,128)(2,1)}, u32[]{:S(2)}, u32[]{:S(2)}) collective-permute-start(bf16[4080,128]{1,0:T(8,128)(2,1)} %collective-permute-done.1.refs_2_), channel_id=1, source_target_pairs={{0,64},{64,0},{1,65},{65,1},{2,66},{66,2},{3,67},{67,3},{4,68},{68... | collective-permute-start | bytes 3133448 | tf_op jit(solution)/shard_map/ppermute | solution.py:790
  210.1 7.1 %collective-permute-start.7 = (bf16[4080,128]{1,0:T(8,128)(2,1)}, bf16[4080,128]{1,0:T(8,128)(2,1)}, u32[]{:S(2)}, u32[]{:S(2)}) collective-permute-start(bf16[4080,128]{1,0:T(8,128)(2,1)} %collective-permute-done.2.refs_3_), channel_id=1, source_target_pairs={{0,64},{64,0},{1,65},{65,1},{2,66},{66,2},{3,67},{67,3},{4,68},{68... | collective-permute-start | bytes 3133448 | tf_op jit(solution)/shard_map/ppermute | solution.py:790
  210.2 27.0 %all-to-all-start.6 = ((bf16[16,320,128]{2,1,0:T(8,128)(2,1)}), bf16[16,320,128]{2,1,0:T(8,128)(2,1)}, u32[]{:S(2)}, u32[]{:S(2)}) async-start(bf16[16,320,128]{2,1,0:T(8,128)(2,1)} %attend_back_second.1), calls=%async_computation.6 | async-start | bytes 2621440 | tf_op jit(solution)/shard_map/all_to_all | solution.py:782
  226.4 23.3 %collective-permute-start.10 = (bf16[4,384,128]{2,1,0:T(8,128)(2,1)}, bf16[4,384,128]{2,1,0:T(8,128)(2,1)}, u32[]{:S(2)}, u32[]{:S(2)}) collective-permute-start(bf16[4,384,128]{2,1,0:T(8,128)(2,1)} %get-tuple-element.125), channel_id=1, source_target_pairs={{0,12},{4,0},{8,4},{12,8},{1,13},{5,1},{9,5},{13,9},{2,14},{6,2},{... | collective-permute-start | bytes 1179656 | tf_op jit(solution)/shard_map/ppermute | solution.py:786
  228.9 20.8 %collective-permute-start.8 = (bf16[4,384,128]{2,1,0:T(8,128)(2,1)}, bf16[4,384,128]{2,1,0:T(8,128)(2,1)}, u32[]{:S(2)}, u32[]{:S(2)}) collective-permute-start(bf16[4,384,128]{2,1,0:T(8,128)(2,1)} %get-tuple-element.124), channel_id=1, source_target_pairs={{0,4},{4,8},{8,12},{12,0},{1,5},{5,9},{9,13},{13,1},{2,6},{6,10},{... | collective-permute-start | bytes 1179656 | tf_op jit(solution)/shard_map/ppermute | solution.py:786
  228.9 23.7 %collective-permute-start.9 = (bf16[4,384,128]{2,1,0:T(8,128)(2,1)}, bf16[4,384,128]{2,1,0:T(8,128)(2,1)}, u32[]{:S(2)}, u32[]{:S(2)}) collective-permute-start(bf16[4,384,128]{2,1,0:T(8,128)(2,1)} %get-tuple-element.126), channel_id=1, source_target_pairs={{0,8},{4,12},{8,0},{12,4},{1,9},{5,13},{9,1},{13,5},{2,10},{6,14},... | collective-permute-start | bytes 1179656 | tf_op jit(solution)/shard_map/ppermute | solution.py:786
  243.4 13.3 %copy-start.5 = (bf16[16,128,128]{2,1,0:T(8,128)(2,1)S(1)}, bf16[16,128,128]{2,1,0:T(8,128)(2,1)}, u32[]{:S(2)}) copy-start(bf16[16,128,128]{2,1,0:T(8,128)(2,1)} %get-tuple-element.95.mine_ref) | copy-start | bytes 1572868
  243.4 13.3 %copy-start.6 = (f32[768,128]{1,0:T(8,128)S(1)}, f32[768,128]{1,0:T(8,128)}, u32[]{:S(2)}) copy-start(f32[768,128]{1,0:T(8,128)} %get-tuple-element.103.dh1_ref) | copy-start | bytes 1179652
  243.4 13.3 %all-to-all-start.7 = ((bf16[4,768,128]{2,1,0:T(8,128)(2,1)}), bf16[4,768,128]{2,1,0:T(8,128)(2,1)S(1)}, u32[]{:S(2)}, u32[]{:S(2)}) async-start(bf16[4,768,128]{2,1,0:T(8,128)(2,1)} %get-tuple-element.97), calls=%async_computation.7 | async-start | bytes 1572864 | tf_op jit(solution)/shard_map/all_to_all | solution.py:782
  247.0 9.6 %collective-permute-start.3 = (bf16[16,128,128]{2,1,0:T(8,128)(2,1)}, bf16[16,128,128]{2,1,0:T(8,128)(2,1)S(1)}, u32[]{:S(2)}, u32[]{:S(2)}) collective-permute-start(bf16[16,128,128]{2,1,0:T(8,128)(2,1)} %get-tuple-element.96), channel_id=1, source_target_pairs={{0,64},{64,0},{1,65},{65,1},{2,66},{66,2},{3,67},{67,3},{4,68},{68... | collective-permute-start | bytes 1572872 | tf_op jit(solution)/shard_map/ppermute | solution.py:790
  257.8 25.4 %all-to-all-start.8 = ((bf16[16,176,128]{2,1,0:T(8,128)(2,1)}), bf16[16,176,128]{2,1,0:T(8,128)(2,1)S(1)}, u32[]{:S(2)}, u32[]{:S(2)}) async-start(bf16[16,176,128]{2,1,0:T(8,128)(2,1)} %last_payload.1), calls=%async_computation.8 | async-start | bytes 1441792 | tf_op jit(solution)/shard_map/all_to_all | solution.py:782
  264.4 13.1 %collective-permute-start.12 = (bf16[384,128]{1,0:T(8,128)(2,1)S(1)}, bf16[384,128]{1,0:T(8,128)(2,1)S(1)}, u32[]{:S(2)}, u32[]{:S(2)}) collective-permute-start(bf16[384,128]{1,0:T(8,128)(2,1)S(1)} %get-tuple-element.107), channel_id=1, source_target_pairs={{0,1},{1,2},{2,3},{3,0},{4,5},{5,6},{6,7},{7,4},{8,9},{9,10},{10,1... | collective-permute-start | bytes 294920 | tf_op jit(solution)/shard_map/ppermute | solution.py:786
  265.7 12.5 %collective-permute-start.13 = (bf16[384,128]{1,0:T(8,128)(2,1)S(1)}, bf16[384,128]{1,0:T(8,128)(2,1)S(1)}, u32[]{:S(2)}, u32[]{:S(2)}) collective-permute-start(bf16[384,128]{1,0:T(8,128)(2,1)S(1)} %get-tuple-element.108), channel_id=1, source_target_pairs={{0,2},{1,3},{2,0},{3,1},{4,6},{5,7},{6,4},{7,5},{8,10},{9,11},{10,... | collective-permute-start | bytes 294920 | tf_op jit(solution)/shard_map/ppermute | solution.py:786
  268.1 10.1 %collective-permute-start.14 = (bf16[384,128]{1,0:T(8,128)(2,1)S(1)}, bf16[384,128]{1,0:T(8,128)(2,1)S(1)}, u32[]{:S(2)}, u32[]{:S(2)}) collective-permute-start(bf16[384,128]{1,0:T(8,128)(2,1)S(1)} %get-tuple-element.109), channel_id=1, source_target_pairs={{0,3},{1,0},{2,1},{3,2},{4,7},{5,4},{6,5},{7,6},{8,11},{9,8},{10,9... | collective-permute-start | bytes 294920 | tf_op jit(solution)/shard_map/ppermute | solution.py:786
  278.3 4.0 %collective-permute-start.15 = (f32[384,128]{1,0:T(8,128)S(1)}, f32[384,128]{1,0:T(8,128)S(1)}, u32[]{:S(2)}, u32[]{:S(2)}) collective-permute-start(f32[384,128]{1,0:T(8,128)S(1)} %convert_add_fusion.1.wide_ref), channel_id=1, source_target_pairs={{0,64},{64,0},{1,65},{65,1},{2,66},{66,2},{3,67},{67,3},{4,68},{68... | collective-permute-start | bytes 589832 | tf_op jit(solution)/shard_map/ppermute | solution.py:790
  283.2 1.4 collective-permute-start.11
  (5 other events, 38.6 us)
Sparse Core Ops, SparseCore 0:
  25.9 94.0 all-gather.2
